TPU v7x, 256 devices: a whole 4x4x8 slice. The times are simulated.
256 devices in a mesh: frame: 32 (over z_hi, y, core), mlp: 8 (over z_lo, x).
Axes of the slice: x: 4, y: 4, z: 8 (z_hi: 4, z_lo: 2; z = z_hi * 2 + z_lo), core: 2. Of those that a mesh axis runs over, the one named last changes fastest.
Arguments:
- tokens: bfloat16 [6, 64, 256, 1024], P(None, 'frame'), may hold values from -8 to 8
- output_gradient: bfloat16 [6, 64, 256, 1024], P(None, 'frame'), may hold values from -6 to 6
- gain: float32 [1024], replicated, may hold values from 0.25 to 1.75
- qkv_weight: bfloat16 [1024, 3, 1024], P(None, None, 'mlp'), may hold values from -1 to 1
- out_weight: bfloat16 [1024, 1024], P('mlp'), may hold values from -0.1875 to 0.1875
Outputs:
- token_gradient: bfloat16 [6, 64, 256, 1024], P(None, 'frame')
- grad_qkv: float32 [1024, 3, 1024], P('frame', None, 'mlp')
- grad_out_weight: float32 [1024, 1024], P('mlp', 'frame')
- gain_gradient: float32 [1024], P('frame')
All inputs are finite; a program needn't handle non-finite values.
Results may differ from a plain program's by a relative error of at most 0.035.
The roundings to bfloat16 on the way count: a program that leaves them out, or rounds other values in their place, can miss the bound.
Values may be sent and summed in bfloat16 or wider, within the bound.
A program may use at most 128 MiB of HBM per device.

v0:
```python
import jax
import jax.numpy as jnp
from jax import lax
from jax.sharding import PartitionSpec as P

HD = 64


def apply_norm(tokens, gain):
    values = tokens.astype(jnp.float32)
    centered_rows = values - jnp.mean(values, axis=-1, keepdims=True)
    inverse_deviation = lax.rsqrt(
        jnp.mean(centered_rows * centered_rows, axis=-1, keepdims=True) + 1e-05
    )
    standardized_input = centered_rows * inverse_deviation
    return (standardized_input, inverse_deviation, (standardized_input * gain).astype(jnp.bfloat16))


def temporal(query, keys, values, d_out, factor):
    f32 = jnp.float32
    scores = jnp.einsum("nfphe,ngphe->nphfg", query, keys, preferred_element_type=f32) * factor
    top = jnp.max(scores, axis=-1, keepdims=True)
    expo = jnp.exp(scores - top)
    probs = expo / jnp.sum(expo, axis=-1, keepdims=True)
    probs_b = probs.astype(jnp.bfloat16)
    attn_out = jnp.einsum("nphfg,ngphe->nfphe", probs_b, values, preferred_element_type=f32).astype(
        jnp.bfloat16
    )
    dprob = jnp.einsum("nfphe,ngphe->nphfg", d_out, values, preferred_element_type=f32)
    d_value = jnp.einsum("nphfg,nfphe->ngphe", probs_b, d_out, preferred_element_type=f32).astype(
        jnp.bfloat16
    )
    delta = jnp.sum(probs * dprob, axis=-1, keepdims=True)
    dscore = (probs * (dprob - delta) * factor).astype(jnp.bfloat16)
    d_query = jnp.einsum("nphfg,ngphe->nfphe", dscore, keys, preferred_element_type=f32).astype(
        jnp.bfloat16
    )
    d_key = jnp.einsum("nphfg,nfphe->ngphe", dscore, query, preferred_element_type=f32).astype(
        jnp.bfloat16
    )
    return (attn_out, d_query, d_key, d_value)


def norm_backward(
    normalized_gradient, standardized_input, inverse_deviation, gain, output_gradient
):
    backward_pass = normalized_gradient * gain
    inner_product = (
        backward_pass
        - jnp.mean(backward_pass, axis=-1, keepdims=True)
        - standardized_input * jnp.mean(backward_pass * standardized_input, axis=-1, keepdims=True)
    )
    return (output_gradient.astype(jnp.float32) + inverse_deviation * inner_product).astype(
        jnp.bfloat16
    )


def shards(tokens, output_gradient, gain, qkv_weight, out_weight):
    clips, fr_loc, patches, width = tokens.shape
    local_cols = out_weight.shape[0]
    heads_loc = local_cols // HD
    standardized_input, inverse_deviation, normalized_rows = apply_norm(tokens, gain)
    rows2 = normalized_rows.reshape(-1, width)
    weight2 = qkv_weight.reshape(width, 3 * local_cols)
    proj = jnp.dot(rows2, weight2, preferred_element_type=jnp.float32).astype(jnp.bfloat16)
    proj = proj.reshape(clips, fr_loc, patches, 3, local_cols)
    grad2 = output_gradient.reshape(-1, width)
    d_attn = jnp.dot(grad2, out_weight.T, preferred_element_type=jnp.float32).astype(jnp.bfloat16)
    d_attn = d_attn.reshape(clips, fr_loc, patches, local_cols)
    parts = (
        lax.all_to_all(proj[:, :, :, 0], "frame", split_axis=2, concat_axis=1, tiled=True),
        lax.all_to_all(proj[:, :, :, 1], "frame", split_axis=2, concat_axis=1, tiled=True),
        lax.all_to_all(proj[:, :, :, 2], "frame", split_axis=2, concat_axis=1, tiled=True),
        lax.all_to_all(d_attn, "frame", split_axis=2, concat_axis=1, tiled=True),
    )
    count, frames, patch_loc, cols = parts[0].shape
    shaped = [piece.reshape(count, frames, patch_loc, heads_loc, HD) for piece in parts]
    results = temporal(shaped[0], shaped[1], shaped[2], shaped[3], HD ** (-0.5))
    flat = [piece.reshape(count, frames, patch_loc, cols) for piece in results]
    attn_out = lax.all_to_all(flat[0], "frame", split_axis=1, concat_axis=2, tiled=True)
    d_query = lax.all_to_all(flat[1], "frame", split_axis=1, concat_axis=2, tiled=True)
    d_key = lax.all_to_all(flat[2], "frame", split_axis=1, concat_axis=2, tiled=True)
    d_value = lax.all_to_all(flat[3], "frame", split_axis=1, concat_axis=2, tiled=True)
    dstack = jnp.stack([d_query, d_key, d_value], axis=3).reshape(-1, 3 * local_cols)
    wo_term = jnp.dot(attn_out.reshape(-1, local_cols).T, grad2, preferred_element_type=jnp.float32)
    d_partial = jnp.dot(dstack, weight2.T, preferred_element_type=jnp.float32).reshape(
        clips, fr_loc, patches, width
    )
    grad_qkv = lax.psum_scatter(
        jnp.dot(rows2.T, dstack, preferred_element_type=jnp.float32)
        .reshape(width // lax.axis_size("frame") * lax.axis_size("frame"), 3, local_cols)
        .astype(jnp.bfloat16),
        "frame",
        scatter_dimension=0,
        tiled=True,
    ).astype(jnp.float32)
    normalized_gradient = lax.psum(d_partial.astype(jnp.bfloat16), "mlp").astype(jnp.float32)
    gain_product = jnp.sum(normalized_gradient * standardized_input, axis=(0, 1, 2))
    token_gradient = norm_backward(
        normalized_gradient, standardized_input, inverse_deviation, gain, output_gradient
    )
    grad_out_weight, gain_sum = (
        lax.psum_scatter(
            wo_term.astype(jnp.bfloat16), "frame", scatter_dimension=1, tiled=True
        ).astype(jnp.float32),
        lax.psum_scatter(
            gain_product[None, :].astype(jnp.bfloat16), "frame", scatter_dimension=1, tiled=True
        ).astype(jnp.float32),
    )
    return (token_gradient, grad_qkv, grad_out_weight, gain_sum[0])


def solution(mesh):
    in_specs = (
        P(None, "frame", None, None),
        P(None, "frame", None, None),
        P(),
        P(None, None, "mlp"),
        P("mlp", None),
    )
    out_specs = (
        P(None, "frame", None, None),
        P("frame", None, "mlp"),
        P("mlp", "frame"),
        P("frame"),
    )
    return jax.shard_map(shards, mesh=mesh, in_specs=in_specs, out_specs=out_specs, check_vma=False)
```

profile of v0, /device:TPU:1, one launch (start us, length us, event | category | flops | bytes accessed | tf_op | source)
XLA Modules:
  0.0 600.6 jit_solution(9111385046257945059)
XLA Ops:
  9.0 4.6 convolution_convert_fusion.1
  15.3 12.8 %all-to-all-start.2 = ((bf16[6,2,256,128]{3,1,0,2:T(2,128)(2,1)}), bf16[6,2,256,128]{3,1,0,2:T(2,128)(2,1)}, u32[]{:S(2)}, u32[]{:S(2)}) async-start(bf16[6,2,256,128]{3,1,0,2:T(2,128)(2,1)} %copy.92), calls=%async_computation.2 | async-start | bytes 1572864 | tf_op jit(solution)/shard_map/all_to_all | solution.py:74
  28.1 3.8 convert_reduce_fusion
  35.1 4.6 fusion.9
  39.7 2.7 copy-done.3
  42.4 3.7 convolution_convert_fusion
  46.1 2.6 copy.83
  48.7 5.6 reshape.101
  54.3 2.6 slice_bitcast_fusion
  56.8 3.7 copy.96
  60.6 9.8 %all-to-all-start.3 = ((bf16[6,2,256,128]{3,1,0,2:T(2,128)(2,1)}), bf16[6,2,256,128]{3,1,0,2:T(2,128)(2,1)S(1)}, u32[]{:S(2)}, u32[]{:S(2)}) async-start(bf16[6,2,256,128]{3,1,0,2:T(2,128)(2,1)} %copy.96), calls=%async_computation.3 | async-start | bytes 1572864 | tf_op jit(solution)/shard_map/all_to_all | solution.py:73
  72.7 20.3 %all-to-all-done.3 = bf16[6,2,256,128]{3,1,0,2:T(2,128)(2,1)S(1)} async-done(((bf16[6,2,256,128]{3,1,0,2:T(2,128)(2,1)}), bf16[6,2,256,128]{3,1,0,2:T(2,128)(2,1)S(1)}, u32[]{:S(2)}, u32[]{:S(2)}) %all-to-all-start.3) | async-done | bytes 786464 | tf_op jit(solution)/shard_map/all_to_all | solution.py:73
  93.0 6.5 %all-to-all-start.1 = ((bf16[6,2,256,128]{3,1,0,2:T(2,128)(2,1)}), bf16[6,2,256,128]{3,1,0,2:T(2,128)(2,1)S(1)}, u32[]{:S(2)}, u32[]{:S(2)}) async-start(bf16[6,2,256,128]{3,1,0,2:T(2,128)(2,1)} %copy.88), calls=%async_computation.1 | async-start | bytes 1572864 | tf_op jit(solution)/shard_map/all_to_all | solution.py:71
  101.9 20.7 %all-to-all-done.1 = bf16[6,2,256,128]{3,1,0,2:T(2,128)(2,1)S(1)} async-done(((bf16[6,2,256,128]{3,1,0,2:T(2,128)(2,1)}), bf16[6,2,256,128]{3,1,0,2:T(2,128)(2,1)S(1)}, u32[]{:S(2)}, u32[]{:S(2)}) %all-to-all-start.1) | async-done | bytes 786464 | tf_op jit(solution)/shard_map/all_to_all | solution.py:71
  122.6 5.5 all-to-all-start
  134.2 3.2 reshape.107
  137.4 3.2 copy.117
  142.8 3.2 reshape.103
  146.0 3.2 copy.105
  153.2 3.2 reshape.102
  156.4 3.3 copy.100
  159.7 3.9 fusion.49
  163.6 4.4 fusion.48
  168.0 7.1 %fusion.32 = bf16[6,8,2,64,64]{4,3,2,1,0:T(8,128)(2,1)} fusion(bf16[6,64,8,2,64]{1,4,3,2,0:T(8,128)(2,1)S(1)} %copy-done.5, f32[6,8,2,64,64]{3,4,2,1,0:T(8,128)} %fusion.49, f32[6,8,2,64,64]{3,4,2,1,0:T(8,128)} %get-tuple-element.11, f32[6,8,2,64]{3,2,1,0:T(2,128)S(1)} %get-tuple-element.10), kind=kOutput, calls=%fused_computation.34 | convolution fusion | flops 53483584 | bytes 4743168 | tf_op jit(solution)/shard_map/nphfg,nfphe->ngphe/dot_general | solution.py:38
  175.1 2.7 copy.107
  177.7 8.0 %all-to-all-start.5 = ((bf16[6,64,8,128]{3,2,0,1:T(8,128)(2,1)}), bf16[6,64,8,128]{3,2,0,1:T(8,128)(2,1)}, u32[]{:S(2)}, u32[]{:S(2)}) async-start(bf16[6,64,8,128]{3,2,0,1:T(8,128)(2,1)} %copy.107), calls=%async_computation.5 | async-start | bytes 1572864 | tf_op jit(solution)/shard_map/all_to_all | solution.py:82
  185.7 7.0 %fusion.29 = bf16[6,8,2,64,64]{4,3,2,1,0:T(8,128)(2,1)} fusion(bf16[6,64,8,2,64]{1,4,3,2,0:T(8,128)(2,1)S(1)} %copy-done.6, f32[6,8,2,64,64]{3,4,2,1,0:T(8,128)} %fusion.49, f32[6,8,2,64,64]{3,4,2,1,0:T(8,128)} %get-tuple-element.11, f32[6,8,2,64]{3,2,1,0:T(2,128)S(1)} %get-tuple-element.10), kind=kOutput, calls=%fused_computation.33 | convolution fusion | flops 53483584 | bytes 4743168 | tf_op jit(solution)/shard_map/nphfg,ngphe->nfphe/dot_general | solution.py:35
  192.7 2.6 copy.102
  195.4 13.3 %all-to-all-done.5 = bf16[6,64,8,128]{3,2,0,1:T(8,128)(2,1)} async-done(((bf16[6,64,8,128]{3,2,0,1:T(8,128)(2,1)}), bf16[6,64,8,128]{3,2,0,1:T(8,128)(2,1)}, u32[]{:S(2)}, u32[]{:S(2)}) %all-to-all-start.5) | async-done | bytes 786464 | tf_op jit(solution)/shard_map/all_to_all | solution.py:82
  208.7 5.2 all-to-all-start.4
  213.9 3.6 convolution_convert_fusion.2
  217.5 2.5 copy.119
  220.1 16.9 %all-to-all-done.4 = bf16[6,64,8,128]{3,2,0,1:T(8,128)(2,1)} async-done(((bf16[6,64,8,128]{3,2,0,1:T(8,128)(2,1)}), bf16[6,64,8,128]{3,2,0,1:T(8,128)(2,1)}, u32[]{:S(2)}, u32[]{:S(2)}) %all-to-all-start.4) | async-done | bytes 786464 | tf_op jit(solution)/shard_map/all_to_all | solution.py:81
  237.0 5.2 all-to-all-start.7
  242.2 4.0 convolution_convert_fusion.3
  248.7 16.4 %all-to-all-done.7 = bf16[6,64,8,128]{3,2,0,1:T(8,128)(2,1)S(1)} async-done(((bf16[6,64,8,128]{3,2,0,1:T(8,128)(2,1)}), bf16[6,64,8,128]{3,2,0,1:T(8,128)(2,1)S(1)}, u32[]{:S(2)}, u32[]{:S(2)}) %all-to-all-start.7) | async-done | bytes 786464 | tf_op jit(solution)/shard_map/all_to_all | solution.py:80
  265.1 5.2 all-to-all-start.6
  274.6 6.0 %convolution_convert_fusion.5 = bf16[128,1024]{0,1:T(8,128)(2,1)} fusion(bf16[3072,128]{1,0:T(8,128)(2,1)S(1)} %bitcast.120, bf16[3072,1024]{1,0:T(8,128)(2,1)} %bitcast.111), kind=kOutput, calls=%fused_computation.42 | convolution fusion | flops 805437440 | bytes 7340032 | tf_op jit(solution)/shard_map/dot_general | solution.py:85
  280.7 12.6 %all-to-all-done.6 = bf16[6,64,8,128]{3,2,0,1:T(8,128)(2,1)S(1)} async-done(((bf16[6,64,8,128]{3,2,0,1:T(8,128)(2,1)}), bf16[6,64,8,128]{3,2,0,1:T(8,128)(2,1)S(1)}, u32[]{:S(2)}, u32[]{:S(2)}) %all-to-all-start.6) | async-done | bytes 786464 | tf_op jit(solution)/shard_map/all_to_all | solution.py:83
  296.1 5.9 copy.115
  302.0 2.9 reshape.111
  304.9 7.2 %convolution_convert_fusion.4 = bf16[1024,3,128]{2,0,1:T(8,128)(2,1)} fusion(bf16[3072,1024,1]{1,0,2:T(8,128)(2,1)} %bitcast.113, bf16[3,128,3072]{2,1,0:T(8,128)(2,1)} %bitcast.129), kind=kOutput, calls=%fused_computation.41 | convolution fusion | flops 2416312320 | bytes 9437184 | tf_op jit(solution)/shard_map/dot_general | solution.py:90
  312.3 5.4 bitcast_convert_fusion
  317.9 73.6 %reduce-scatter.8.cloned.1.call-done = bf16[128,32]{0,1:T(8,128)(2,1)} async-done(((bf16[128,1024]{0,1:T(8,128)(2,1)}), bf16[128,32]{0,1:T(8,128)(2,1)}) %reduce-scatter.8.cloned.1.call-update) | async-done | bytes 8208 | tf_op jit(solution)/shard_map/reduce_scatter | solution.py:103
  392.8 101.6 %reduce-scatter.6.cloned.1.call-done = bf16[32,3,128]{2,0,1:T(8,128)(2,1)} async-done(((bf16[1024,3,128]{2,0,1:T(8,128)(2,1)}), bf16[32,3,128]{2,0,1:T(8,128)(2,1)}) %reduce-scatter.6.cloned.1.call-update) | async-done | bytes 24592 | tf_op jit(solution)/shard_map/reduce_scatter | solution.py:89
  495.8 9.3 %fusion.16 = (bf16[1024]{0:T(1024)(128)(2,1)S(1)}, f32[6,2,256]{2,1,0:T(2,128)S(1)}, f32[6,2,256]{2,1,0:T(2,128)S(1)}) fusion(bf16[6,2,256,1024]{3,2,1,0:T(8,128)(2,1)} %param.5, bf16[6,2,256,1024]{3,2,1,0:T(8,128)(2,1)} %all-reduce.2.cloned.1.call-done, f32[6,2,256]{2,1,0:T(2,128)S(1)} %add_rsqrt_fusion, f32[6,2,256]{2,1,0:T(2,128)S(1)} %broadcast_multiply_fusion.2, ...), kind=kLoop, calls=%fused_computation.20 | loop fusion | flops 31450112 | bytes 12638208 | tf_op jit(solution)/shard_map/reduce_sum | solution.py:98
  506.1 12.0 %fusion.13 = bf16[6,2,256,1024]{3,2,1,0:T(8,128)(2,1)} fusion(bf16[6,2,256,1024]{3,2,1,0:T(8,128)(2,1)} %param.5, bf16[6,2,256,1024]{3,2,1,0:T(8,128)(2,1)} %all-reduce.2.cloned.1.call-done, bf16[6,2,256,1024]{3,2,1,0:T(8,128)(2,1)} %param.6, f32[6,2,256]{2,1,0:T(2,128)S(1)} %get-tuple-element.12, f32[6,2,256]{2,1,0:T(2,128)S(1)} %get-tuple-element.13, ...), kind=kLoop, calls=%fused_computation.17 | loop fusion | flops 37748736 | bytes 25219072 | tf_op jit(solution)/shard_map/convert_element_type | solution.py:53
  518.1 73.8 %reduce-scatter.10.cloned.1.call-done = bf16[32,1]{1,0:T(8,128)(2,1)} async-done(((bf16[1024,1]{1,0:T(8,128)(2,1)}), bf16[32,1]{1,0:T(8,128)(2,1)}) %reduce-scatter.10.cloned.1.call-update) | async-done | bytes 80
  (72 shorter events, 37.5 us)
Async XLA Ops:
  8.0 1.0 copy-start
  15.3 45.3 %all-to-all-start.2 = ((bf16[6,2,256,128]{3,1,0,2:T(2,128)(2,1)}), bf16[6,2,256,128]{3,1,0,2:T(2,128)(2,1)}, u32[]{:S(2)}, u32[]{:S(2)}) async-start(bf16[6,2,256,128]{3,1,0,2:T(2,128)(2,1)} %copy.92), calls=%async_computation.2 | async-start | bytes 1572864 | tf_op jit(solution)/shard_map/all_to_all | solution.py:74
  28.1 4.6 copy-start.2
  32.7 2.1 copy-start.15
  32.7 2.4 copy-start.17
  39.7 2.7 copy-start.3
  56.8 13.5 %copy-start.11 = (bf16[6,2,256,128]{2,1,0,3:T(2,128)(2,1)S(1)}, bf16[6,2,256,128]{2,1,0,3:T(2,128)(2,1)}, u32[]{:S(2)}) copy-start(bf16[6,2,256,128]{2,1,0,3:T(2,128)(2,1)} %get-tuple-element.8) | copy-start | bytes 2359300
  60.6 32.5 %all-to-all-start.3 = ((bf16[6,2,256,128]{3,1,0,2:T(2,128)(2,1)}), bf16[6,2,256,128]{3,1,0,2:T(2,128)(2,1)S(1)}, u32[]{:S(2)}, u32[]{:S(2)}) async-start(bf16[6,2,256,128]{3,1,0,2:T(2,128)(2,1)} %copy.96), calls=%async_computation.3 | async-start | bytes 1572864 | tf_op jit(solution)/shard_map/all_to_all | solution.py:73
  93.0 36.3 %copy-start.12 = (bf16[6,2,256,128]{3,1,0,2:T(2,128)(2,1)}, bf16[6,2,256,128]{3,1,0,2:T(2,128)(2,1)S(1)}, u32[]{:S(2)}) copy-start(bf16[6,2,256,128]{3,1,0,2:T(2,128)(2,1)S(1)} %all-to-all-done.3) | copy-start | bytes 2359300
  93.0 29.6 %all-to-all-start.1 = ((bf16[6,2,256,128]{3,1,0,2:T(2,128)(2,1)}), bf16[6,2,256,128]{3,1,0,2:T(2,128)(2,1)S(1)}, u32[]{:S(2)}, u32[]{:S(2)}) async-start(bf16[6,2,256,128]{3,1,0,2:T(2,128)(2,1)} %copy.88), calls=%async_computation.1 | async-start | bytes 1572864 | tf_op jit(solution)/shard_map/all_to_all | solution.py:71
  122.6 6.8 %copy-start.13 = (bf16[6,2,256,128]{3,1,0,2:T(2,128)(2,1)}, bf16[6,2,256,128]{3,1,0,2:T(2,128)(2,1)S(1)}, u32[]{:S(2)}) copy-start(bf16[6,2,256,128]{3,1,0,2:T(2,128)(2,1)S(1)} %all-to-all-done.1) | copy-start | bytes 2359300
  122.6 28.5 %all-to-all-start = ((bf16[6,2,256,128]{3,1,0,2:T(2,128)(2,1)}), bf16[6,2,256,128]{3,1,0,2:T(2,128)(2,1)}, u32[]{:S(2)}, u32[]{:S(2)}) async-start(bf16[6,2,256,128]{3,1,0,2:T(2,128)(2,1)} %copy.85), calls=%async_computation | async-start | bytes 1572864 | tf_op jit(solution)/shard_map/all_to_all | solution.py:72
  159.7 3.9 copy-start.5
  175.1 10.6 %copy-start.6 = (bf16[6,64,8,2,64]{1,4,3,2,0:T(8,128)(2,1)S(1)}, bf16[6,64,8,2,64]{1,4,3,2,0:T(8,128)(2,1)}, u32[]{:S(2)}) copy-start(bf16[6,64,8,2,64]{1,4,3,2,0:T(8,128)(2,1)} %copy.100) | copy-start | bytes 2359300
  177.7 31.0 %all-to-all-start.5 = ((bf16[6,64,8,128]{3,2,0,1:T(8,128)(2,1)}), bf16[6,64,8,128]{3,2,0,1:T(8,128)(2,1)}, u32[]{:S(2)}, u32[]{:S(2)}) async-start(bf16[6,64,8,128]{3,2,0,1:T(8,128)(2,1)} %copy.107), calls=%async_computation.5 | async-start | bytes 1572864 | tf_op jit(solution)/shard_map/all_to_all | solution.py:82
  192.7 21.2 %copy-start.4 = (bf16[6,64,8,2,64]{1,4,3,2,0:T(8,128)(2,1)S(1)}, bf16[6,64,8,2,64]{1,4,3,2,0:T(8,128)(2,1)}, u32[]{:S(2)}) copy-start(bf16[6,64,8,2,64]{1,4,3,2,0:T(8,128)(2,1)} %copy.117) | copy-start | bytes 2359300
  208.7 28.3 %all-to-all-start.4 = ((bf16[6,64,8,128]{3,2,0,1:T(8,128)(2,1)}), bf16[6,64,8,128]{3,2,0,1:T(8,128)(2,1)}, u32[]{:S(2)}, u32[]{:S(2)}) async-start(bf16[6,64,8,128]{3,2,0,1:T(8,128)(2,1)} %copy.102), calls=%async_computation.4 | async-start | bytes 1572864 | tf_op jit(solution)/shard_map/all_to_all | solution.py:81
  237.0 28.1 %all-to-all-start.7 = ((bf16[6,64,8,128]{3,2,0,1:T(8,128)(2,1)}), bf16[6,64,8,128]{3,2,0,1:T(8,128)(2,1)S(1)}, u32[]{:S(2)}, u32[]{:S(2)}) async-start(bf16[6,64,8,128]{3,2,0,1:T(8,128)(2,1)} %copy.119), calls=%async_computation.8 | async-start | bytes 1572864 | tf_op jit(solution)/shard_map/all_to_all | solution.py:80
  265.1 7.9 %copy-start.14 = (bf16[6,64,8,128]{3,2,0,1:T(8,128)(2,1)}, bf16[6,64,8,128]{3,2,0,1:T(8,128)(2,1)S(1)}, u32[]{:S(2)}) copy-start(bf16[6,64,8,128]{3,2,0,1:T(8,128)(2,1)S(1)} %all-to-all-done.7) | copy-start | bytes 2359300
  265.1 28.2 %all-to-all-start.6 = ((bf16[6,64,8,128]{3,2,0,1:T(8,128)(2,1)}), bf16[6,64,8,128]{3,2,0,1:T(8,128)(2,1)S(1)}, u32[]{:S(2)}, u32[]{:S(2)}) async-start(bf16[6,64,8,128]{3,2,0,1:T(8,128)(2,1)} %copy.112), calls=%async_computation.6 | async-start | bytes 1572864 | tf_op jit(solution)/shard_map/all_to_all | solution.py:83
  270.3 121.2 %reduce-scatter.8.cloned.1.call-start = ((), (), s32[]{:S(2)}) async-start(), calls=%async_computation.13 | async-start | bytes 270336 | tf_op jit(solution)/shard_map/reduce_scatter | solution.py:103
  273.0 20.5 %copy-start.7 = (bf16[6,2,32,8,128]{4,3,2,1,0:T(8,128)(2,1)}, bf16[6,2,32,8,128]{4,3,2,1,0:T(8,128)(2,1)S(1)}, u32[]{:S(2)}) copy-start(bf16[6,2,32,8,128]{4,3,2,1,0:T(8,128)(2,1)S(1)} %copy.151) | copy-start | bytes 2359300
  280.7 213.7 %reduce-scatter.6.cloned.1.call-start = ((), (), s32[]{:S(2)}) async-start(), calls=%async_computation.12 | async-start | bytes 811008 | tf_op jit(solution)/shard_map/reduce_scatter | solution.py:89
  293.5 0.9 copy-start.9
  304.9 7.3 %copy-start.8 = (bf16[6,2,32,8,128]{4,3,2,1,0:T(8,128)(2,1)S(1)}, bf16[6,2,32,8,128]{4,3,2,1,0:T(8,128)(2,1)}, u32[]{:S(2)}) copy-start(bf16[6,2,32,8,128]{4,3,2,1,0:T(8,128)(2,1)} %copy-done.7) | copy-start | bytes 2359300
  304.9 7.3 %copy-start.10 = (bf16[6,2,32,8,128]{4,3,2,1,0:T(8,128)(2,1)S(1)}, bf16[6,2,32,8,128]{4,3,2,1,0:T(8,128)(2,1)}, u32[]{:S(2)}) copy-start(bf16[6,2,32,8,128]{4,3,2,1,0:T(8,128)(2,1)} %copy-done.9) | copy-start | bytes 2359300
  304.9 7.3 %copy-start.16 = (bf16[1024,3,128]{2,0,1:T(8,128)(2,1)S(1)}, bf16[1024,3,128]{2,0,1:T(8,128)(2,1)}, u32[]{:S(2)}) copy-start(bf16[1024,3,128]{2,0,1:T(8,128)(2,1)} %param.8) | copy-start | bytes 2359300
  312.2 183.6 %all-reduce.2.cloned.1.call-start = ((), (), s32[]{:S(2)}) async-start(), calls=%async_computation.11 | async-start | bytes 12582912 | tf_op jit(solution)/shard_map/psum | solution.py:97
  317.6 274.3 %reduce-scatter.10.cloned.1.call-start = ((), (), s32[]{:S(2)}) async-start(), calls=%async_computation.14 | async-start | bytes 270336
  506.1 87.2 %copy-start.1 = (bf16[128,1024]{1,0:T(8,128)(2,1)S(1)}, bf16[128,1024]{1,0:T(8,128)(2,1)}, u32[]{:S(2)}) copy-start(bf16[128,1024]{1,0:T(8,128)(2,1)} %param.9) | copy-start | bytes 786436
Sparse Core Ops, SparseCore 0:
  280.8 110.6 reduce-scatter.7
  395.3 99.1 reduce-scatter.5
  506.1 85.7 reduce-scatter.9
Sparse Core Ops, SparseCore 1:
  317.7 148.6 all-reduce.1
where the time goes:
time: 612 us; the launch traced here: 601 us
  waiting for transfers between devices  351 us (57%)
  local copies, waits for them, and re-layouts  81.4 us (13%)
  starting transfers between devices  58.5 us (10%)
  matrix products  56.8 us (9%)
  other arithmetic  36.8 us (6%)
  between operations  15.8 us (3%)
    reduce_scatter x1, waiting for transfers between devices, shards(): lax.psum_scatter(jnp.dot(rows2.T, dstack, preferred_element_type=jnp.floa...  102 us
    unnamed x5, waiting for transfers between devices  73.9 us
    reduce_scatter x1, waiting for transfers between devices, shards(): lax.psum_scatter(wo_term.astype(jnp.bfloat16), 'frame', scatter_dimension...  73.6 us
    reshape x8, local copies, waits for them, and re-layouts, shards(): piece.reshape(count, frames, patch_loc, heads_loc, HD)  21.8 us
    all_to_all x1, waiting for transfers between devices, shards(): lax.all_to_all(proj[:, :, :, 0], 'frame', split_axis=2, concat_axis=1, ti...  20.7 us
    all_to_all x1, waiting for transfers between devices, shards(): lax.all_to_all(proj[:, :, :, 2], 'frame', split_axis=2, concat_axis=1, ti...  20.3 us
    all_to_all x1, waiting for transfers between devices, shards(): lax.all_to_all(flat[1], 'frame', split_axis=1, concat_axis=2, tiled=True)  16.9 us
    all_to_all x1, waiting for transfers between devices, shards(): lax.all_to_all(flat[0], 'frame', split_axis=1, concat_axis=2, tiled=True)  16.4 us
  transfers between devices with their start and end apart: 12, of which 10 were waited for; matrix products, arithmetic and copies ran while one was open for 21% of the time, Pallas kernels for 0%

commit v1 on v0

v1 whole, which is shorter than its diff:
```python
import functools

import numpy as np

import jax
import jax.numpy as jnp
from jax import lax
from jax.experimental import pallas as pl
from jax.experimental.pallas import tpu as pltpu
from jax.sharding import PartitionSpec as P

MESH = pl.DeviceIdType.MESH
BF = jnp.bfloat16
F32 = jnp.float32
D = 1024
FACTOR = 64 ** (-0.5)
NEG = -1e30


def one_hot(shape, perm):
    index = np.arange(384).reshape(shape).transpose(perm).reshape(-1)
    return np.eye(384, dtype=np.float32)[index]


PACK = one_hot((2, 12, 8, 2), (2, 0, 3, 1))
GROUP = one_hot((8, 2, 12, 2), (1, 2, 0, 3))
REPACK = one_hot((2, 12, 8, 2), (2, 0, 1, 3))
UNPACK = one_hot((8, 2, 2, 12), (1, 3, 0, 2))


def place():
    f, m = lax.axis_index("frame"), lax.axis_index("mlp")
    return f, m, f // 2, f % 2, m // 4, m % 4


def remote(src, dst, send, recv, f, m):
    return pltpu.make_async_remote_copy(
        src_ref=src, dst_ref=dst, send_sem=send, recv_sem=recv, device_id=(f, m), device_id_type=MESH
    )


def greet(barrier, f, m):
    pl.semaphore_signal(barrier, inc=1, device_id=(f, m), device_id_type=MESH)


def scatter_kernel(
    tok, og, wc, perm, recv, wout, xin, sbuf, loc, wloc, asend, arecv, fsend, frecv, ssend, srecv, rsend, rrecv
):
    f, m, g, c, z, x = place()
    sib = g * 2 + 1 - c
    pf, pm = g * 2 + 1 - c, (1 - z) * 4 + x
    mr, ml = z * 4 + (x + 1) % 4, z * 4 + (x + 3) % 4
    xl, xr, xf = (x + 3) % 4, (x + 1) % 4, (x + 2) % 4
    rows = pl.ds(pl.multiple_of(m * 32, 32), 32)
    in_tok = pltpu.make_async_copy(tok.at[:, rows, :], xin.at[0], loc.at[0])
    in_og = pltpu.make_async_copy(og.at[:, rows, :], xin.at[1], loc.at[1])
    in_tok.start()
    in_og.start()

    barrier = pltpu.get_barrier_semaphore()

    def hello(k, _):
        greet(barrier, ((g + k) % 16) * 2 + c, m)
        return 0

    lax.fori_loop(1, 16, hello, 0)
    greet(barrier, sib, m)
    greet(barrier, pf, pm)
    greet(barrier, f, mr)
    greet(barrier, f, ml)
    pl.semaphore_wait(barrier, 19)

    halves = (pl.ds(0, 512), pl.ds(512, 512))

    def ring(src, slot, h, i, mm):
        return remote(src, wout.at[slot, halves[h]], rsend.at[i], rrecv.at[i], f, mm)

    own = c == z
    own_copy = pltpu.make_async_copy(wc, wout.at[x], wloc)

    def swap(h):
        return remote(wc.at[halves[h]], wout.at[x, halves[h]], ssend.at[h], srecv.at[h], pf, pm)

    @pl.when(own)
    def _():
        ring(wc.at[halves[0]], x, 0, 0, mr).start()
        ring(wc.at[halves[1]], x, 1, 2, ml).start()
        ring(wc.at[halves[1]], x, 1, 1, mr).start()
        ring(wc.at[halves[0]], x, 0, 3, ml).start()
        own_copy.start()

    @pl.when(jnp.logical_not(own))
    def _():
        swap(0).start()
        swap(1).start()

    in_tok.wait()
    in_og.wait()
    for gh in range(2):
        block = xin[:, :, 16 * gh : 16 * gh + 16, :].reshape(384, D)
        packed = jnp.dot(perm[...], block, preferred_element_type=F32).astype(BF)
        sbuf[8 * gh : 8 * gh + 8] = packed.reshape(8, 48, D)

    def a2a(k):
        return remote(sbuf.at[(g + k) % 16], recv.at[c, g], asend.at[k], arecv.at[k], ((g + k) % 16) * 2 + c, m)

    def send(k, _):
        a2a(k).start()
        return 0

    lax.fori_loop(1, 16, send, 0)
    keep = pltpu.make_async_copy(sbuf.at[g], recv.at[c, g], loc.at[2])
    keep.start()

    def forward(k, src):
        slot = (g + 16 - k) % 16
        return remote(src, recv.at[c, slot], fsend.at[k], frecv.at[k], sib, m)

    forward(0, sbuf.at[g]).start()

    @pl.when(jnp.logical_not(own))
    def _():
        swap(0).wait_recv()
        ring(wout.at[x, halves[0]], x, 0, 0, mr).start()
        ring(wout.at[x, halves[0]], x, 0, 3, ml).start()
        swap(1).wait_recv()
        ring(wout.at[x, halves[1]], x, 1, 2, ml).start()
        ring(wout.at[x, halves[1]], x, 1, 1, mr).start()

    def relay(k, _):
        slot = (g + 16 - k) % 16
        remote(sbuf.at[0], recv.at[c, slot], asend.at[k], arecv.at[k], f, m).wait_recv()
        forward(k, recv.at[c, slot]).start()
        return 0

    def arrived(slot, h, i):
        ring(wout.at[slot, halves[h]], slot, h, i, mr).wait_recv()

    lax.fori_loop(1, 9, relay, 0)
    arrived(xl, 0, 0)
    ring(wout.at[xl, halves[0]], xl, 0, 4, mr).start()
    arrived(xr, 1, 2)
    ring(wout.at[xr, halves[1]], xr, 1, 5, ml).start()
    lax.fori_loop(9, 16, relay, 0)
    arrived(xl, 1, 1)
    arrived(xr, 0, 3)
    arrived(xf, 0, 4)
    arrived(xf, 1, 5)

    def finish(k, _):
        slot = (g + 16 - k) % 16
        a2a(k).wait_send()
        forward(k, recv.at[c, slot]).wait_send()
        remote(sbuf.at[0], recv.at[1 - c, slot], fsend.at[k], frecv.at[k], sib, m).wait_recv()
        return 0

    lax.fori_loop(1, 16, finish, 0)
    forward(0, sbuf.at[g]).wait_send()
    remote(sbuf.at[0], recv.at[1 - c, g], fsend.at[0], frecv.at[0], sib, m).wait_recv()
    keep.wait()
    for i, (slot, h) in enumerate(((x, 0), (x, 1), (x, 1), (x, 0), (xl, 0), (xr, 1))):
        ring(wout.at[slot, halves[h]], slot, h, i, mr).wait_send()

    @pl.when(own)
    def _():
        own_copy.wait()

    @pl.when(jnp.logical_not(own))
    def _():
        swap(0).wait_send()
        swap(1).wait_send()


def scatter(tok, og, wc, perm):
    any_spec = pl.BlockSpec(memory_space=pl.ANY)
    dma = pltpu.SemaphoreType.DMA
    return pl.pallas_call(
        scatter_kernel,
        out_shape=(jax.ShapeDtypeStruct((2, 16, 48, D), BF), jax.ShapeDtypeStruct((4, D, 512), BF)),
        in_specs=[any_spec, any_spec, any_spec, pl.BlockSpec(memory_space=pltpu.VMEM)],
        out_specs=(any_spec, any_spec),
        scratch_shapes=[
            pltpu.VMEM((2, 12, 32, D), BF),
            pltpu.VMEM((16, 48, D), BF),
            dma((3,)),
            dma,
            dma((16,)),
            dma((16,)),
            dma((16,)),
            dma((16,)),
            dma((2,)),
            dma((2,)),
            dma((6,)),
            dma((6,)),
        ],
        compiler_params=pltpu.CompilerParams(
            collective_id=0, has_side_effects=True, vmem_limit_bytes=32 * 2**20
        ),
        name="scatter",
    )(tok, og, wc, perm)


def standardize(values):
    centered = values - jnp.mean(values, axis=-1, keepdims=True)
    rstd = lax.rsqrt(jnp.mean(centered * centered, axis=-1, keepdims=True) + 1e-05)
    return centered * rstd, rstd


def dot_t(a, b):
    return lax.dot_general(a, b, (((1,), (1,)), ((), ())), preferred_element_type=F32)


def t_dot(a, b):
    return lax.dot_general(a, b, (((0,), (0,)), ((), ())), preferred_element_type=F32)


def attend(q, k, v, d, allowed, first):
    zero = jnp.zeros_like(k)
    k2 = jnp.concatenate([jnp.where(first, k, zero), jnp.where(first, zero, k)], axis=0)
    v2 = jnp.concatenate([jnp.where(first, v, zero), jnp.where(first, zero, v)], axis=0)
    scores = dot_t(q, k2) * FACTOR
    dprob = dot_t(d, v2)
    probs, dscore = [], []
    for h in range(2):
        s = jnp.where(allowed, scores[:, 128 * h : 128 * h + 128], NEG)
        e = jnp.exp(s - jnp.max(s, axis=-1, keepdims=True))
        p = e * (1.0 / jnp.sum(e, axis=-1, keepdims=True))
        dp = dprob[:, 128 * h : 128 * h + 128]
        delta = jnp.sum(p * dp, axis=-1, keepdims=True)
        probs.append(p.astype(BF))
        dscore.append((p * (dp - delta) * FACTOR).astype(BF))
    probs = jnp.concatenate(probs, axis=1)
    dscore = jnp.concatenate(dscore, axis=1)
    out = jnp.dot(probs, v2, preferred_element_type=F32)
    dq = jnp.dot(dscore, k2, preferred_element_type=F32)
    dv = t_dot(probs, d)
    dk = t_dot(dscore, q)
    dv = jnp.where(first, dv[:128], dv[128:])
    dk = jnp.where(first, dk[:128], dk[128:])
    return out, dq, dk, dv


def core_kernel(recv, w, gain, perm, grads, mine, other, xown, xs, normed, norm_t, og_t, acc, proj, back):
    _, _, _, c, _, _ = place()
    for s in range(2):
        for gh in range(2):
            block = recv[s, 8 * gh : 8 * gh + 8].reshape(384, D)
            rows = jnp.dot(perm[...], block, preferred_element_type=F32).astype(BF)
            xs[:, :, s, 16 * gh : 16 * gh + 16, :] = rows.reshape(2, 12, 16, D)

    xown[...] = xs[:, :, c]

    def norm(u, _):
        values = xs[0, u].reshape(64, D).astype(F32)
        xhat, _ = standardize(values)
        normed[pl.ds(pl.multiple_of(u * 64, 64), 64), :] = (xhat * gain[...]).astype(BF)
        return 0

    lax.fori_loop(0, 12, norm, 0)

    for i in range(6):
        norm_t[:, 128 * i : 128 * i + 128] = normed[128 * i : 128 * i + 128, :].T
        og_t[:, 128 * i : 128 * i + 128] = xs[1, 2 * i : 2 * i + 2].reshape(128, D).T

    acc[...] = jnp.zeros_like(acc)
    lane = lax.broadcasted_iota(jnp.int32, (128, 128), 1)
    line = lax.broadcasted_iota(jnp.int32, (128, 128), 0)
    first = lane < 64
    allowed = (lane < 64) == (line < 64)

    def group(j, _):
        def project(i, _):
            rows = pl.ds(pl.multiple_of(i * 256, 256), 256)
            proj[rows, 0:384] = jnp.dot(normed[rows, :], w[j, :, 0:384], preferred_element_type=F32).astype(BF)
            cot = xs[1, pl.ds(i * 4, 4)].reshape(256, D)
            proj[rows, 384:512] = jnp.dot(cot, w[j, :, 384:512], preferred_element_type=F32).astype(BF)
            return 0

        lax.fori_loop(0, 3, project, 0)

        def pair(i, _):
            for e in range(2):
                rows = pl.ds(pl.multiple_of(i * 256 + e * 128, 128), 128)
                out, dq, dk, dv = attend(
                    proj[rows, 0:128], proj[rows, 128:256], proj[rows, 256:384], proj[rows, 384:512], allowed, first
                )
                back[rows, 0:128] = dq.astype(BF)
                back[rows, 128:256] = dk.astype(BF)
                back[rows, 256:384] = dv.astype(BF)
                back[rows, 384:512] = out.astype(BF)
            return 0

        lax.fori_loop(0, 3, pair, 0)

        def partial(i, _):
            rows = pl.ds(pl.multiple_of(i * 128, 128), 128)
            term = dot_t(back[rows, 0:384], w[j, :, 0:384])
            acc[pl.ds(i * 2, 2)] += term.astype(BF).astype(F32).reshape(2, 2, 32, D)
            return 0

        lax.fori_loop(0, 6, partial, 0)

        def weight(i, _):
            rows = pl.ds(pl.multiple_of(i * 256, 256), 256)
            grads[j, rows, 0:384] = jnp.dot(norm_t[rows, :], back[:, 0:384], preferred_element_type=F32).astype(BF)
            grads[j, rows, 384:512] = jnp.dot(og_t[rows, :], back[:, 384:512], preferred_element_type=F32).astype(BF)
            return 0

        lax.fori_loop(0, 4, weight, 0)
        return 0

    lax.fori_loop(0, 4, group, 0)
    mine[...] = acc[:, c]
    other[...] = acc[:, 1 - c].astype(BF)


def core(recv, w, gain, perm):
    vm = pl.BlockSpec(memory_space=pltpu.VMEM)
    return pl.pallas_call(
        core_kernel,
        out_shape=(
            jax.ShapeDtypeStruct((4, D, 512), BF),
            jax.ShapeDtypeStruct((12, 32, D), F32),
            jax.ShapeDtypeStruct((12, 32, D), BF),
            jax.ShapeDtypeStruct((2, 12, 32, D), BF),
        ),
        in_specs=[vm] * 4,
        out_specs=(vm,) * 4,
        scratch_shapes=[
            pltpu.VMEM((2, 12, 2, 32, D), BF),
            pltpu.VMEM((768, D), BF),
            pltpu.VMEM((D, 768), BF),
            pltpu.VMEM((D, 768), BF),
            pltpu.VMEM((12, 2, 32, D), F32),
            pltpu.VMEM((768, 512), BF),
            pltpu.VMEM((768, 512), BF),
        ],
        compiler_params=pltpu.CompilerParams(vmem_limit_bytes=52 * 2**20),
        name="core",
    )(recv, w, gain, perm)


def gather_kernel(
    mine, other, xown, gain, grads, repack, unpack, tgrad, wgrad,
    rsib, tg, gvec, gvecr, gcol, sbuf, rbuf, blk, gyr, ggr, gz, gzr, gxs, gxr,
    loc, bsend, brecv, vsend, vrecv, ysend, yrecv, gsend, grecv, asend, arecv,
    psend, precv, rsend, rrecv, zsend, zrecv, xsend, xrecv,
):
    f, m, g, c, z, x = place()
    zh, y = f // 8, (f // 2) % 4
    zi = zh * 2 + z
    sib = g * 2 + 1 - c
    pm = (1 - z) * 4 + x
    mr, ml = z * 4 + (x + 1) % 4, z * 4 + (x + 3) % 4
    xl, xr, xf = (x + 3) % 4, (x + 1) % 4, (x + 2) % 4
    barrier = pltpu.get_barrier_semaphore()

    def hello_frame(k, _):
        greet(barrier, ((g + k) % 16) * 2 + c, m)
        return 0

    def hello_column(k, _):
        dz = (zi + k // 2) % 8
        dc = (c + k) % 2
        greet(barrier, ((dz // 2) * 4 + y) * 2 + dc, (dz % 2) * 4 + x)
        return 0

    lax.fori_loop(1, 16, hello_frame, 0)
    lax.fori_loop(1, 16, hello_column, 0)
    for k in range(1, 4):
        greet(barrier, f, z * 4 + (x + k) % 4)
    pl.semaphore_wait(barrier, 33)

    to_sib = remote(other, rsib, bsend, brecv, sib, m)
    to_sib.start()

    def y_copy(k):
        yk = (y + k) % 4
        return remote(
            grads.at[:, :, yk], gyr.at[k], ysend.at[k], yrecv.at[k], (zh * 4 + yk) * 2 + c, m
        )

    for k in (1, 3, 2):
        y_copy(k).start()
    own_y = pltpu.make_async_copy(grads.at[:, :, y], gyr.at[0], loc.at[0])
    own_y.start()

    to_sib.wait_recv()

    def token(u, total):
        xhat, rstd = standardize(xown[0, u].astype(F32))
        dn = mine[u] + rsib[u].astype(F32)
        bp = dn * gain[...]
        inner = bp - jnp.mean(bp, axis=-1, keepdims=True) - xhat * jnp.mean(bp * xhat, axis=-1, keepdims=True)
        tg[u] = (xown[1, u].astype(F32) + rstd * inner).astype(BF)
        return total + jnp.sum((dn * xhat).reshape(4, 8, D), axis=0)

    total = lax.fori_loop(0, 12, token, jnp.zeros((8, D), F32))
    gvec[...] = jnp.broadcast_to(jnp.sum(total, axis=0, keepdims=True), (8, D))
    to_sib_gain = remote(gvec, gvecr, vsend, vrecv, sib, m)
    to_sib_gain.start()

    for gh in range(2):
        halves = [tg[:, 16 * gh : 16 * gh + 16, 512 * h : 512 * h + 512].reshape(192, 512) for h in range(2)]
        packed = jnp.dot(repack[...], jnp.concatenate(halves, axis=0), preferred_element_type=F32)
        sbuf[8 * gh : 8 * gh + 8] = packed.astype(BF).reshape(8, 48, 512)

    def a2a(k):
        return remote(sbuf.at[(g + k) % 16], rbuf.at[g], asend.at[k], arecv.at[k], ((g + k) % 16) * 2 + c, m)

    def send(k, _):
        a2a(k).start()
        return 0

    lax.fori_loop(1, 16, send, 0)
    keep = pltpu.make_async_copy(sbuf.at[g], rbuf.at[g], loc.at[1])
    keep.start()

    to_sib_gain.wait_recv()
    column = jnp.broadcast_to(gvec[0:1] + gvecr[0:1], (128, D)).T
    gcol[...] = column.astype(BF).reshape(4, 4, 2, 32, 128)

    def gain_copy(k):
        yk = (y + k) % 4
        return remote(gcol.at[:, yk], ggr.at[k], gsend.at[k], grecv.at[k], (zh * 4 + yk) * 2 + c, m)

    for k in range(1, 4):
        gain_copy(k).start()
    own_gain = pltpu.make_async_copy(gcol.at[:, y], ggr.at[0], loc.at[2])
    own_gain.start()

    keep.wait()

    def received(k, _):
        remote(sbuf.at[0], rbuf.at[(g + 16 - k) % 16], asend.at[k], arecv.at[k], f, m).wait_recv()
        return 0

    lax.fori_loop(1, 16, received, 0)
    for gh in range(2):
        rows = jnp.dot(unpack[...], rbuf[8 * gh : 8 * gh + 8].reshape(384, 512), preferred_element_type=F32)
        rows = rows.astype(BF).reshape(2, 12, 16, 512)
        for h in range(2):
            blk[:, 16 * gh : 16 * gh + 16, 512 * h : 512 * h + 512] = rows[h]

    def span(mm):
        return pl.ds(pl.multiple_of(mm * 32, 32), 32)

    six = (pl.ds(0, 6), pl.ds(6, 6))

    def part(mm, h):
        return tgrad.at[six[h], span(mm), :]

    def pair(h):
        return remote(blk.at[six[h]], part(m, h), psend.at[h], precv.at[h], f, pm)

    def ring(r, src, mm, h, i, to):
        return remote(src, part(mm, h), rsend.at[r, i], rrecv.at[r, i], f, to)

    pair(0).start()
    pair(1).start()
    ring(0, blk.at[six[0]], m, 0, 0, mr).start()
    ring(0, blk.at[six[1]], m, 1, 2, ml).start()
    ring(0, blk.at[six[1]], m, 1, 1, mr).start()
    ring(0, blk.at[six[0]], m, 0, 3, ml).start()
    own_out = pltpu.make_async_copy(blk, tgrad.at[:, span(m), :], loc.at[3])
    own_out.start()

    def pair_arrived(h):
        remote(blk.at[six[h]], part(pm, h), psend.at[h], precv.at[h], f, pm).wait_recv()

    pair_arrived(0)
    ring(1, part(pm, 0), pm, 0, 0, mr).start()
    ring(1, part(pm, 0), pm, 0, 3, ml).start()
    pair_arrived(1)
    ring(1, part(pm, 1), pm, 1, 2, ml).start()
    ring(1, part(pm, 1), pm, 1, 1, mr).start()

    def arrived(r, mm, h, i):
        ring(r, part(mm, h), mm, h, i, mr).wait_recv()

    def base(r):
        return (z if r == 0 else 1 - z) * 4

    def relay(r):
        arrived(r, base(r) + xl, 0, 0)
        ring(r, part(base(r) + xl, 0), base(r) + xl, 0, 4, mr).start()
        arrived(r, base(r) + xr, 1, 2)
        ring(r, part(base(r) + xr, 1), base(r) + xr, 1, 5, ml).start()

    relay(0)

    own_y.wait()
    own_gain.wait()
    for k in range(1, 4):
        remote(gyr.at[0], gyr.at[k], ysend.at[k], yrecv.at[k], f, m).wait_recv()
        remote(ggr.at[0], ggr.at[k], gsend.at[k], grecv.at[k], f, m).wait_recv()

    def sum_y(n, _):
        a, b = n // 2, n % 2
        for j in range(4):
            terms = [gyr[k, j, a, b].astype(F32) for k in range(4)]
            gz[a, b, :, 512 * j : 512 * j + 512] = ((terms[0] + terms[1]) + (terms[2] + terms[3])).astype(BF)
        terms = [ggr[k, a, b].astype(F32) for k in range(4)]
        gz[a, b, :, 2048:2176] = ((terms[0] + terms[1]) + (terms[2] + terms[3])).astype(BF)
        return 0

    lax.fori_loop(0, 8, sum_y, 0)

    def z_copy(n):
        return remote(
            gz.at[n // 2, n % 2], gzr.at[zi], zsend.at[n], zrecv.at[zi], ((n // 2) * 4 + y) * 2 + n % 2, c * 4 + x
        )

    def z_self(n):
        return jnp.logical_and(n == zh * 2 + c, c == z)

    def z_send(n, _):
        @pl.when(jnp.logical_not(z_self(n)))
        def _():
            z_copy(n).start()

        return 0

    lax.fori_loop(0, 8, z_send, 0)
    own_z = pltpu.make_async_copy(gz.at[zh, c], gzr.at[zi], loc.at[4])

    @pl.when(c == z)
    def _():
        own_z.start()

    relay(1)

    def z_wait(n, _):
        @pl.when(jnp.logical_not(jnp.logical_and(n == zi, c == z)))
        def _():
            remote(gz.at[0, 0], gzr.at[n], zsend.at[0], zrecv.at[n], f, m).wait_recv()

        return 0

    lax.fori_loop(0, 8, z_wait, 0)

    @pl.when(c == z)
    def _():
        own_z.wait()

    for j in range(5):
        cols = slice(512 * j, 512 * j + (512 if j < 4 else 128))
        terms = [gzr[k, :, cols].astype(F32) for k in range(8)]
        while len(terms) > 1:
            terms = [a + b for a, b in zip(terms[::2], terms[1::2])]
        if j < 4:
            gxs[j, :, 0:512] = terms[0].astype(BF)
        else:
            for i in range(4):
                gxs[i, :, 512:640] = terms[0].astype(BF)

    def x_copy(k):
        xk = (x + k) % 4
        return remote(gxs.at[xk], gxr.at[k], xsend.at[k], xrecv.at[k], f, z * 4 + xk)

    for k in range(1, 4):
        x_copy(k).start()
    for k in range(1, 4):
        remote(gxs.at[0], gxr.at[k], xsend.at[k], xrecv.at[k], f, m).wait_recv()
    wgrad[...] = (gxs[x].astype(F32) + gxr[1].astype(F32)) + (gxr[2].astype(F32) + gxr[3].astype(F32))

    for r in range(2):
        arrived(r, base(r) + xl, 1, 1)
        arrived(r, base(r) + xr, 0, 3)
        arrived(r, base(r) + xf, 0, 4)
        arrived(r, base(r) + xf, 1, 5)
        for i, (mm, h) in enumerate(((x, 0), (x, 1), (x, 1), (x, 0), (xl, 0), (xr, 1))):
            ring(r, part(base(r) + mm, h), base(r) + mm, h, i, mr).wait_send()
    pair(0).wait_send()
    pair(1).wait_send()
    own_out.wait()
    to_sib.wait_send()
    to_sib_gain.wait_send()

    def a2a_sent(k, _):
        a2a(k).wait_send()
        return 0

    lax.fori_loop(1, 16, a2a_sent, 0)
    for k in range(1, 4):
        y_copy(k).wait_send()
        gain_copy(k).wait_send()
        x_copy(k).wait_send()

    def z_sent(n, _):
        @pl.when(jnp.logical_not(z_self(n)))
        def _():
            z_copy(n).wait_send()

        return 0

    lax.fori_loop(0, 8, z_sent, 0)


def gather(mine, other, xown, gain, grads, repack, unpack):
    vm = pl.BlockSpec(memory_space=pltpu.VMEM)
    any_spec = pl.BlockSpec(memory_space=pl.ANY)
    dma = pltpu.SemaphoreType.DMA
    return pl.pallas_call(
        gather_kernel,
        out_shape=(jax.ShapeDtypeStruct((12, 256, D), BF), jax.ShapeDtypeStruct((32, 640), F32)),
        in_specs=[vm, any_spec, vm, vm, any_spec, vm, vm],
        out_specs=(any_spec, vm),
        scratch_shapes=[
            pltpu.VMEM((12, 32, D), BF),
            pltpu.VMEM((12, 32, D), BF),
            pltpu.VMEM((8, D), F32),
            pltpu.VMEM((8, D), F32),
            pltpu.VMEM((4, 4, 2, 32, 128), BF),
            pltpu.VMEM((16, 48, 512), BF),
            pltpu.VMEM((16, 48, 512), BF),
            pltpu.VMEM((12, 32, D), BF),
            pltpu.VMEM((4, 4, 4, 2, 32, 512), BF),
            pltpu.VMEM((4, 4, 2, 32, 128), BF),
            pltpu.VMEM((4, 2, 32, 2176), BF),
            pltpu.VMEM((8, 32, 2176), BF),
            pltpu.VMEM((4, 32, 640), BF),
            pltpu.VMEM((4, 32, 640), BF),
            dma((5,)),
            dma,
            dma,
            dma,
            dma,
            dma((4,)),
            dma((4,)),
            dma((4,)),
            dma((4,)),
            dma((16,)),
            dma((16,)),
            dma((2,)),
            dma((2,)),
            dma((2, 6)),
            dma((2, 6)),
            dma((8,)),
            dma((8,)),
            dma((4,)),
            dma((4,)),
        ],
        compiler_params=pltpu.CompilerParams(
            collective_id=1, has_side_effects=True, vmem_limit_bytes=48 * 2**20
        ),
        name="gather",
    )(mine, other, xown, gain, grads, repack, unpack)


def shards(tokens, output_gradient, gain, qkv_weight, out_weight):
    clips, frames, patches, width = tokens.shape
    tok = tokens.reshape(12, 256, D)
    og = output_gradient.reshape(12, 256, D)
    wc = jnp.concatenate([qkv_weight.reshape(D, 384), out_weight.T], axis=1)
    gain_row = gain.reshape(1, D)
    recv, w = scatter(tok, og, wc, jnp.asarray(PACK, BF))
    grads, mine, other, xown = core(recv, w, gain_row, jnp.asarray(GROUP, BF))
    tgrad, wgrad = gather(
        mine,
        other,
        xown,
        gain_row,
        grads.reshape(4, 4, 4, 2, 32, 512),
        jnp.asarray(REPACK, BF),
        jnp.asarray(UNPACK, BF),
    )
    return (
        tgrad.reshape(clips, frames, patches, width),
        wgrad[:, 0:384].reshape(32, 3, 128),
        wgrad[:, 384:512].T,
        wgrad[:, 512],
    )


def solution(mesh):
    in_specs = (
        P(None, "frame", None, None),
        P(None, "frame", None, None),
        P(),
        P(None, None, "mlp"),
        P("mlp", None),
    )
    out_specs = (
        P(None, "frame", None, None),
        P("frame", None, "mlp"),
        P("mlp", "frame"),
        P("frame"),
    )
    return jax.shard_map(shards, mesh=mesh, in_specs=in_specs, out_specs=out_specs, check_vma=False)
```

time: 612 us -> 255 us (0.42); the launches traced: 601 us -> 255 us
  waiting for transfers between devices: 351 us -> 0 us
  Pallas kernels: 0 us -> 231 us
  starting transfers between devices: 58.5 us -> 0 us
  local copies, waits for them, and re-layouts: 81.4 us -> 23 us
  matrix products: 56.8 us -> 0 us
  other arithmetic: 36.8 us -> 0.09 us
  between operations: 15.8 us -> 0.72 us
    pallas_call x0 -> x3, Pallas kernels: none -> 231 us  [the longest x1 120 us: gather(): pl.pallas_call(gather_kernel, out_shape=(jax.ShapeDtypeStruct((12, 256, D...]
    reduce_scatter x2 -> x0, waiting for transfers between devices: 175 us -> none  [the longest x1 102 us: shards(): lax.psum_scatter(jnp.dot(rows2.T, dstack, preferred_element_type=jnp.floa...]
    all_to_all x8 -> x0, waiting for transfers between devices: 102 us -> none  [the longest x1 20.7 us: shards(): lax.all_to_all(proj[:, :, :, 0], 'frame', split_axis=2, concat_axis=1, ti...]
    unnamed x5 -> x0, waiting for transfers between devices: 73.9 us -> none
    all_to_all x8 -> x0, starting transfers between devices: 58.1 us -> none  [the longest x1 12.8 us: shards(): lax.all_to_all(d_attn, 'frame', split_axis=2, concat_axis=1, tiled=True)]
    dot_general x10 -> x0, matrix products: 52.4 us -> none  [the longest x1 7.25 us: shards(): jnp.dot(rows2.T, dstack, preferred_element_type=jnp.float32)]
    reshape x15 -> x1, local copies, waits for them, and re-layouts: 42.4 us -> 0.35 us  [shards(): wc = jnp.concatenate([qkv_weight.reshape(D, 384), out_weight.T], axis=1)]
    convert_element_type x4 -> x0, other arithmetic: 19.3 us -> none  [the longest x1 12 us: norm_backward(): (output_gradient.astype(jnp.float32) + inverse_deviation * inner_product)...]
  transfers between devices with their start and end apart: 12 -> 0, of which waited for: 10 -> 0; matrix products, arithmetic and copies ran while one was open for 21% -> 0% of each run, Pallas kernels for 0% -> 0%
where the time goes in v1:
time: 255 us
  Pallas kernels  231 us (91%)
  local copies, waits for them, and re-layouts  23 us (9%)
    pallas_call x1, Pallas kernels, gather(): pl.pallas_call(gather_kernel, out_shape=(jax.ShapeDtypeStruct((12, 256, D...  120 us
    pallas_call x1, Pallas kernels, scatter(): pl.pallas_call(scatter_kernel, out_shape=(jax.ShapeDtypeStruct((2, 16, 48...  63.4 us
    pallas_call x1, Pallas kernels, core(): pl.pallas_call(core_kernel, out_shape=(jax.ShapeDtypeStruct((4, D, 512),...  47.9 us
    unnamed x26, local copies, waits for them, and re-layouts  21.4 us

profile of v1, /device:TPU:1, one launch (start us, length us, event | category | flops | bytes accessed | tf_op | source)
XLA Modules:
  0.0 254.8 jit_solution(4033947196946313214)
XLA Ops:
  0.6 0.0 copy-start.9
  0.6 1.2 copy.17
  1.8 1.4 copy.16
  3.2 0.4 copy.18
  3.6 0.1 pad_maximum_fusion.wc
  3.7 0.0 copy-done.9
  3.7 0.0 copy-start
  3.7 2.8 %copy-done = bf16[6,2,256,1024]{3,2,1,0:T(8,128)(2,1)S(1)} copy-done((bf16[6,2,256,1024]{3,2,1,0:T(8,128)(2,1)S(1)}, bf16[6,2,256,1024]{3,2,1,0:T(8,128)(2,1)}, u32[]{:S(2)}) %copy-start) | copy-done | bytes 6291480
  6.5 0.0 copy-start.1
  6.5 2.8 %copy-done.1 = bf16[6,2,256,1024]{3,2,1,0:T(8,128)(2,1)S(1)} copy-done((bf16[6,2,256,1024]{3,2,1,0:T(8,128)(2,1)S(1)}, bf16[6,2,256,1024]{3,2,1,0:T(8,128)(2,1)}, u32[]{:S(2)}) %copy-start.1) | copy-done | bytes 6291480
  9.3 0.0 copy-start.8
  9.3 0.0 copy-start.10
  9.3 63.4 %scatter.1 = (bf16[2,16,48,1024]{3,2,1,0:T(8,128)(2,1)S(1)}, bf16[4,1024,512]{2,1,0:T(8,128)(2,1)S(1)}) custom-call(bf16[12,256,1024]{2,1,0:T(8,128)(2,1)S(1)} %bitcast.14, bf16[12,256,1024]{2,1,0:T(8,128)(2,1)S(1)} %bitcast.15, bf16[1024,512]{1,0:T(8,128)(2,1)S(1)} %pad_maximum_fusion.wc, bf16[384,384]{1,0:T(8,128)(2,1)S(1)} %copy-done.9), custom_call_target="tpu_custom_call" | custom-call | tf_op jit(solution)/shard_map/scatter/pallas_call | solution.py:177
  72.7 0.0 copy-start.2
  72.7 2.0 copy-done.2
  74.7 0.0 copy-start.3
  74.7 1.6 copy-done.3
  76.3 0.0 copy-start.6
  76.3 0.0 copy-start.7
  76.3 0.0 copy-done.8
  76.3 0.0 copy-done.10
  76.3 47.9 %core.1 = (bf16[4,1024,512]{2,1,0:T(8,128)(2,1)}, f32[12,32,1024]{2,1,0:T(8,128)}, bf16[12,32,1024]{2,1,0:T(8,128)(2,1)S(1)}, bf16[2,12,32,1024]{3,2,1,0:T(8,128)(2,1)}) custom-call(bf16[2,16,48,1024]{3,2,1,0:T(8,128)(2,1)} %copy-done.3, bf16[4,1024,512]{2,1,0:T(8,128)(2,1)} %copy-done.2, f32[1,1024]{1,0:T(1,128)S(1)} %bitcast.16, bf16[384,384]{1,0:T(8,128)(2,1)S(1)} %copy-done.8), custom_call_target="tpu_custom_call" | custom-call | tf_op jit(solution)/shard_map/core/pallas_call | solution.py:319
  124.3 0.0 copy-done.6
  124.3 0.0 copy-done.7
  124.3 0.0 copy-start.4
  124.3 1.4 copy-done.4
  125.7 0.0 copy-start.5
  125.7 1.4 copy-done.5
  127.1 119.6 %gather.1 = (bf16[12,256,1024]{2,1,0:T(8,128)(2,1)}, f32[32,640]{1,0:T(8,128)S(1)}) custom-call(f32[12,32,1024]{2,1,0:T(8,128)S(1)} %copy-done.4, bf16[12,32,1024]{2,1,0:T(8,128)(2,1)S(1)} %get-tuple-element.15.other, bf16[2,12,32,1024]{3,2,1,0:T(8,128)(2,1)S(1)} %copy-done.5, f32[1,1024]{1,0:T(1,128)S(1)} %bitcast.17, ...), custom_call_target="tpu_custom_call" | custom-call | tf_op jit(solution)/shard_map/gather/pallas_call | solution.py:604
  246.7 0.6 slice_reduce_fusion
  247.4 0.6 slice_bitcast_fusion.1
  248.0 0.6 copy_bitcast_fusion
  248.6 6.2 %copy.23 = bf16[6,2,256,1024]{3,2,1,0:T(8,128)(2,1)} copy(bf16[6,2,256,1024]{3,2,1,0:T(8,128)(2,1)} %bitcast.18) | data formatting | bytes 12582912
Async XLA Ops:
  0.6 3.1 %copy-start.9 = (bf16[384,384]{1,0:T(8,128)(2,1)S(1)}, bf16[384,384]{1,0:T(8,128)(2,1)}, u32[]{:S(2)}) copy-start(bf16[384,384]{1,0:T(8,128)(2,1)} %constant.8.clone.perm) | copy-start | bytes 884740
  3.7 2.8 %copy-start = (bf16[6,2,256,1024]{3,2,1,0:T(8,128)(2,1)S(1)}, bf16[6,2,256,1024]{3,2,1,0:T(8,128)(2,1)}, u32[]{:S(2)}) copy-start(bf16[6,2,256,1024]{3,2,1,0:T(8,128)(2,1)} %param.9) | copy-start | bytes 18874372
  6.5 2.8 %copy-start.1 = (bf16[6,2,256,1024]{3,2,1,0:T(8,128)(2,1)S(1)}, bf16[6,2,256,1024]{3,2,1,0:T(8,128)(2,1)}, u32[]{:S(2)}) copy-start(bf16[6,2,256,1024]{3,2,1,0:T(8,128)(2,1)} %param.10) | copy-start | bytes 18874372
  9.3 67.0 %copy-start.8 = (bf16[384,384]{1,0:T(8,128)(2,1)S(1)}, bf16[384,384]{1,0:T(8,128)(2,1)}, u32[]{:S(2)}) copy-start(bf16[384,384]{1,0:T(8,128)(2,1)} %constant.9.clone.perm) | copy-start | bytes 884740
  9.3 67.0 %copy-start.10 = (f32[1024]{0:T(1024)S(1)}, f32[1024]{0:T(1024)}, u32[]{:S(2)}) copy-start(f32[1024]{0:T(1024)} %param.11) | copy-start | bytes 12292
  72.7 2.0 copy-start.2
  74.7 1.6 copy-start.3
  76.3 48.0 %copy-start.6 = (bf16[384,384]{1,0:T(8,128)(2,1)S(1)}, bf16[384,384]{1,0:T(8,128)(2,1)}, u32[]{:S(2)}) copy-start(bf16[384,384]{1,0:T(8,128)(2,1)} %constant.11.clone.unpack) | copy-start | bytes 884740
  76.3 48.0 %copy-start.7 = (bf16[384,384]{1,0:T(8,128)(2,1)S(1)}, bf16[384,384]{1,0:T(8,128)(2,1)}, u32[]{:S(2)}) copy-start(bf16[384,384]{1,0:T(8,128)(2,1)} %constant.10.clone.repack) | copy-start | bytes 884740
  124.3 1.4 copy-start.4
  125.7 1.4 copy-start.5

commit v2 on v0

v2 whole, which is shorter than its diff:
```python
import numpy as np

import jax
import jax.numpy as jnp
from jax import lax
from jax.experimental import pallas as pl
from jax.experimental.pallas import tpu as pltpu
from jax.sharding import PartitionSpec as P

MESH = pl.DeviceIdType.MESH
BF = jnp.bfloat16
F32 = jnp.float32
D = 1024
FACTOR = 64 ** (-0.5)
NEG = -1e30


def one_hot(shape, perm):
    index = np.arange(384).reshape(shape).transpose(perm).reshape(-1)
    return np.eye(384, dtype=np.float32)[index]


PACK = one_hot((2, 2, 6, 8, 2), (3, 0, 1, 4, 2))
GROUP = one_hot((8, 2, 2, 6, 2), (1, 2, 3, 0, 4))
REPACK = one_hot((4, 6, 8, 2), (2, 0, 1, 3))
UNPACK = one_hot((8, 4, 2, 6), (1, 3, 0, 2))


def remote(src, dst, send, recv, f, m):
    return pltpu.make_async_remote_copy(
        src_ref=src, dst_ref=dst, send_sem=send, recv_sem=recv, device_id=(f, m), device_id_type=MESH
    )


def greet(barrier, f, m):
    pl.semaphore_signal(barrier, inc=1, device_id=(f, m), device_id_type=MESH)


def standardize(values):
    centered = values - jnp.mean(values, axis=-1, keepdims=True)
    rstd = lax.rsqrt(jnp.mean(centered * centered, axis=-1, keepdims=True) + 1e-05)
    return centered * rstd, rstd


def dot_t(a, b):
    return lax.dot_general(a, b, (((1,), (1,)), ((), ())), preferred_element_type=F32)


def t_dot(a, b):
    return lax.dot_general(a, b, (((0,), (0,)), ((), ())), preferred_element_type=F32)


def attend(q, k, v, d, allowed, first):
    zero = jnp.zeros_like(k)
    k2 = jnp.concatenate([jnp.where(first, k, zero), jnp.where(first, zero, k)], axis=0)
    v2 = jnp.concatenate([jnp.where(first, v, zero), jnp.where(first, zero, v)], axis=0)
    scores = dot_t(q, k2) * FACTOR
    dprob = dot_t(d, v2)
    probs, dscore = [], []
    for h in range(2):
        s = jnp.where(allowed, scores[:, 128 * h : 128 * h + 128], NEG)
        e = jnp.exp(s - jnp.max(s, axis=-1, keepdims=True))
        p = e * (1.0 / jnp.sum(e, axis=-1, keepdims=True))
        dp = dprob[:, 128 * h : 128 * h + 128]
        delta = jnp.sum(p * dp, axis=-1, keepdims=True)
        probs.append(p.astype(BF))
        dscore.append((p * (dp - delta) * FACTOR).astype(BF))
    probs = jnp.concatenate(probs, axis=1)
    dscore = jnp.concatenate(dscore, axis=1)
    out = jnp.dot(probs, v2, preferred_element_type=F32)
    dq = jnp.dot(dscore, k2, preferred_element_type=F32)
    dv = t_dot(probs, d)
    dk = t_dot(dscore, q)
    dv = jnp.where(first, dv[:128], dv[128:])
    dk = jnp.where(first, dk[:128], dk[128:])
    return out, dq, dk, dv


def sublayer_kernel(
    tok, og, qkvw, outw, gain, pack_p, group_p, repack_p, unpack_p,
    tgrad, gq, go, gg,
    xin, sbuf, recv, wown, wout, wt, ow, xs, normed, norm_t, og_t, proj, back, ao, part, other, rsib,
    tg, gacc, gvec, gvecr, gcol, sret, rret, blk, grads, gf, gn, ggr, gz, gzr, gzg, gzgr, gxs, gxr, gxg, gxgr,
    loc, kloc, wloc, oloc, zloc, gloc,
    asend, arecv, fsend, frecv, ssend, srecv, wsend, wrecv, bsend, brecv, vsend, vrecv,
    csend, crecv, psend, precv, rsend, rrecv, y1send, y1recv, y2send, y2recv, gsend, grecv,
    zsend, zrecv, xsend, xrecv, hsend, hrecv,
):
    f, m = lax.axis_index("frame"), lax.axis_index("mlp")
    g, c, z, x = f // 2, f % 2, m // 4, m % 4
    zh, y = f // 8, (f // 2) % 4
    zi = zh * 2 + z
    sib = g * 2 + 1 - c
    mz = (1 - z) * 4 + x
    xl, xr, xf = (x + 3) % 4, (x + 1) % 4, (x + 2) % 4
    mr, ml = z * 4 + xr, z * 4 + xl
    yl, yr, yf = (y + 3) % 4, (y + 1) % 4, (y + 2) % 4
    fr, fl = (zh * 4 + yr) * 2 + c, (zh * 4 + yl) * 2 + c
    own = c == z
    rows32 = pl.ds(pl.multiple_of(m * 32, 32), 32)

    w_in = [pltpu.make_async_copy(qkvw.at[j], wown.at[:, pl.ds(128 * j, 128)], loc.at[4 + j]) for j in range(3)]
    w_in.append(pltpu.make_async_copy(outw, ow, loc.at[7]))
    for copy in w_in:
        copy.start()
    x_in = []
    for ch in range(2):
        for t, ref in enumerate((tok, og)):
            x_in.append(
                pltpu.make_async_copy(ref.at[pl.ds(6 * ch, 6), rows32, :], xin.at[ch, t], loc.at[2 * ch + t])
            )
            x_in[-1].start()

    barrier = pltpu.get_barrier_semaphore()

    def hello_frame(k, _):
        greet(barrier, ((g + k) % 16) * 2 + c, m)
        return 0

    def hello_column(k, _):
        dz = (zi + k // 2) % 8
        greet(barrier, ((dz // 2) * 4 + y) * 2 + (c + k) % 2, (dz % 2) * 4 + x)
        return 0

    lax.fori_loop(1, 16, hello_frame, 0)
    lax.fori_loop(1, 16, hello_column, 0)
    for k in range(1, 4):
        greet(barrier, f, z * 4 + (x + k) % 4)

    for copy in w_in:
        copy.wait()
    wown[:, 384:512] = ow[...].T
    pl.semaphore_wait(barrier, 33)

    half = (pl.ds(0, 512), pl.ds(512, 512))
    w_pairs = ((1, 0), (1, 1), (2, 1), (2, 0), (3, 0), (3, 1))

    def w_ring(src, slot, n, to):
        i, h = w_pairs[n]
        return remote(src, wout.at[slot, half[h]], wsend.at[n], wrecv.at[i, h], f, to)

    def w_spread(src, h):
        if h == 0:
            w_ring(src.at[half[0]], x, 0, mr).start()
            w_ring(src.at[half[0]], x, 3, ml).start()
        else:
            w_ring(src.at[half[1]], x, 2, ml).start()
            w_ring(src.at[half[1]], x, 1, mr).start()

    far = (zi + 7 + 2 * z) % 8
    near_id = (g * 2 + 1 - c, mz)
    far_id = (((far // 2) * 4 + y) * 2 + 1 - c, (far % 2) * 4 + x)

    def swap(h):
        return remote(
            wown.at[half[h]], wout.at[x, half[h]], ssend.at[h], srecv.at[h], *(near_id if h == 0 else far_id)
        )

    own_w = pltpu.make_async_copy(wown, wout.at[x], wloc)

    @pl.when(own)
    def _():
        w_spread(wown, 0)
        w_spread(wown, 1)
        own_w.start()

    @pl.when(jnp.logical_not(own))
    def _():
        swap(0).start()
        swap(1).start()

    def a2a(ch, k):
        to = (g + k) % 16
        return remote(sbuf.at[ch, to], recv.at[ch, c, g], asend.at[ch, k], arecv.at[ch, k], to * 2 + c, m)

    def forward(ch, k, src):
        slot = (g + 16 - k) % 16
        return remote(src, recv.at[ch, c, slot], fsend.at[ch, k], frecv.at[ch, k], sib, m)

    def keep(ch):
        return pltpu.make_async_copy(sbuf.at[ch, g], recv.at[ch, c, g], kloc.at[ch])

    for ch in range(2):
        x_in[2 * ch].wait()
        x_in[2 * ch + 1].wait()
        for gh in range(2):
            rows = slice(16 * gh, 16 * gh + 16)
            parts = [xin[ch, t, :, rows, 512 * h : 512 * h + 512].reshape(96, 512) for h in range(2) for t in range(2)]
            packed = jnp.dot(pack_p[...], jnp.concatenate(parts, axis=0), preferred_element_type=F32)
            sbuf[ch, 8 * gh : 8 * gh + 8] = packed.astype(BF).reshape(8, 48, 512)

        def send(k, _, ch=ch):
            a2a(ch, k).start()
            return 0

        lax.fori_loop(1, 16, send, 0)
        keep(ch).start()
        forward(ch, 0, sbuf.at[ch, g]).start()

    @pl.when(jnp.logical_not(own))
    def _():
        swap(0).wait_recv()
        w_spread(wout.at[x], 0)
        swap(1).wait_recv()
        w_spread(wout.at[x], 1)

    def w_arrived(n):
        i, h = w_pairs[n]
        slot = (x, xl, xr, xf)[i]
        remote(wown.at[half[h]], wout.at[slot, half[h]], wsend.at[n], wrecv.at[i, h], f, mr).wait_recv()

    def relay_tokens(ch):
        def relay(k, _):
            slot = (g + 16 - k) % 16
            remote(sbuf.at[ch, 0], recv.at[ch, c, slot], asend.at[ch, k], arecv.at[ch, k], f, m).wait_recv()
            forward(ch, k, recv.at[ch, c, slot]).start()
            return 0

        lax.fori_loop(1, 16, relay, 0)

    def tokens_arrived(ch):
        keep(ch).wait()

        def wait(k, _):
            slot = (g + 16 - k) % 16
            remote(sbuf.at[ch, 0], recv.at[ch, 1 - c, slot], fsend.at[ch, k], frecv.at[ch, k], f, m).wait_recv()
            return 0

        lax.fori_loop(0, 16, wait, 0)

    relay_tokens(0)
    w_arrived(0)
    w_ring(wout.at[xl, half[0]], xl, 4, mr).start()
    w_arrived(2)
    w_ring(wout.at[xr, half[1]], xr, 5, ml).start()

    lane = lax.broadcasted_iota(jnp.int32, (128, 128), 1)
    line = lax.broadcasted_iota(jnp.int32, (128, 128), 0)
    first = lane < 64
    allowed = (lane < 64) == (line < 64)

    def shard_of(i):
        return (x + (i % 2) * 3 + (i // 2) * (1 + (i % 2) * 2)) % 4

    def prepare(ch):
        for s in range(2):
            for gh in range(2):
                block = recv[ch, s, 8 * gh : 8 * gh + 8].reshape(384, 512)
                rows = jnp.dot(group_p[...], block, preferred_element_type=F32).astype(BF).reshape(2, 2, 6, 16, 512)
                for h in range(2):
                    xs[ch, :, :, s, 16 * gh : 16 * gh + 16, 512 * h : 512 * h + 512] = rows[h]

        def norm(u, _):
            xhat, _ = standardize(xs[ch, 0, u].reshape(64, D).astype(F32))
            normed[pl.ds(pl.multiple_of(ch * 384 + u * 64, 64), 64), :] = (xhat * gain[...]).astype(BF)
            return 0

        lax.fori_loop(0, 6, norm, 0)
        for i in range(3):
            at = 384 * ch + 128 * i
            norm_t[:, at : at + 128] = normed[at : at + 128, :].T
            og_t[:, at : at + 128] = xs[ch, 1, 2 * i : 2 * i + 2].reshape(128, D).T

    def heads(ch, i):
        j = shard_of(i)
        at = 384 * ch
        if ch == 0:
            wt[i] = wout[j, :, 0:384].T
        proj[:, 0:384] = jnp.dot(normed[at : at + 384, :], wout[j, :, 0:384], preferred_element_type=F32).astype(BF)
        proj[:, 384:512] = jnp.dot(
            xs[ch, 1].reshape(384, D), wout[j, :, 384:512], preferred_element_type=F32
        ).astype(BF)
        for n in range(3):
            rows = slice(128 * n, 128 * n + 128)
            out, dq, dk, dv = attend(
                proj[rows, 0:128], proj[rows, 128:256], proj[rows, 256:384], proj[rows, 384:512], allowed, first
            )
            rows = slice(at + 128 * n, at + 128 * n + 128)
            back[i, rows, 0:128] = dq.astype(BF)
            back[i, rows, 128:256] = dk.astype(BF)
            back[i, rows, 256:384] = dv.astype(BF)
            ao[i, rows, :] = out.astype(BF)

    def to_sibling(ch):
        return remote(other.at[ch], rsib.at[ch], bsend.at[ch], brecv.at[ch], sib, m)

    def partial(ch):
        for n in range(3):
            rows = slice(384 * ch + 128 * n, 384 * ch + 128 * n + 128)
            term = jnp.dot(back[0, rows, :], wt[0], preferred_element_type=F32)
            for i in range(1, 4):
                term += jnp.dot(back[i, rows, :], wt[i], preferred_element_type=F32)
            part[2 * n : 2 * n + 2] = term.reshape(2, 2, 32, D)
        other[ch] = part[:, 1 - c].astype(BF)
        to_sibling(ch).start()

    def back_to(ch, k):
        to = (g + k) % 16
        return remote(sret.at[ch, to], rret.at[ch, g], csend.at[ch, k], crecv.at[ch, k], to * 2 + c, m)

    def keep_back(ch):
        return pltpu.make_async_copy(sret.at[ch, g], rret.at[ch, g], kloc.at[2 + ch])

    def token_gradient(ch):
        to_sibling(ch).wait_recv()

        def token(u, total):
            xhat, rstd = standardize(xs[ch, 0, u, c].astype(F32))
            dn = part[u, c] + rsib[ch, u].astype(F32)
            bp = dn * gain[...]
            inner = bp - jnp.mean(bp, axis=-1, keepdims=True) - xhat * jnp.mean(bp * xhat, axis=-1, keepdims=True)
            tg[u] = (xs[ch, 1, u, c].astype(F32) + rstd * inner).astype(BF)
            return total + jnp.sum((dn * xhat).reshape(4, 8, D), axis=0)

        total = lax.fori_loop(0, 6, token, jnp.zeros((8, D), F32))
        if ch == 0:
            gacc[...] = total
        else:
            gacc[...] += total
        for gh in range(2):
            rows = slice(16 * gh, 16 * gh + 16)
            parts = [tg[:, rows, 256 * h : 256 * h + 256].reshape(96, 256) for h in range(4)]
            packed = jnp.dot(repack_p[...], jnp.concatenate(parts, axis=0), preferred_element_type=F32)
            sret[ch, 8 * gh : 8 * gh + 8] = packed.astype(BF).reshape(8, 48, 256)

        def send(k, _):
            back_to(ch, k).start()
            return 0

        lax.fori_loop(1, 16, send, 0)
        keep_back(ch).start()

    def span(mm):
        return pl.ds(pl.multiple_of(mm * 32, 32), 32)

    def piece(ch, h, mm):
        return tgrad.at[pl.ds(6 * ch + 3 * h, 3), span(mm), :]

    def pair(ch, h):
        return remote(
            blk.at[ch, pl.ds(3 * h, 3)], piece(ch, h, m), psend.at[ch, h], precv.at[ch, h], f, mz
        )

    def ring(ch, r, src, mm, h, n, to):
        return remote(src, piece(ch, h, mm), rsend.at[ch, r, n], rrecv.at[ch, r, n], f, to)

    def own_out(ch):
        return pltpu.make_async_copy(blk.at[ch], tgrad.at[pl.ds(6 * ch, 6), span(m), :], oloc.at[ch])

    def gather_own(ch):
        keep_back(ch).wait()

        def received(k, _):
            slot = (g + 16 - k) % 16
            remote(sret.at[ch, 0], rret.at[ch, slot], csend.at[ch, k], crecv.at[ch, k], f, m).wait_recv()
            return 0

        lax.fori_loop(1, 16, received, 0)
        for gh in range(2):
            block = rret[ch, 8 * gh : 8 * gh + 8].reshape(384, 256)
            rows = jnp.dot(unpack_p[...], block, preferred_element_type=F32).astype(BF).reshape(4, 6, 16, 256)
            for h in range(4):
                blk[ch, :, 16 * gh : 16 * gh + 16, 256 * h : 256 * h + 256] = rows[h]
        pair(ch, 0).start()
        pair(ch, 1).start()
        mine = [blk.at[ch, pl.ds(3 * h, 3)] for h in range(2)]
        ring(ch, 0, mine[0], m, 0, 0, mr).start()
        ring(ch, 0, mine[1], m, 1, 2, ml).start()
        ring(ch, 0, mine[1], m, 1, 1, mr).start()
        ring(ch, 0, mine[0], m, 0, 3, ml).start()
        own_out(ch).start()

    def gather_pair(ch):
        def arrived(h):
            remote(
                blk.at[ch, pl.ds(3 * h, 3)], piece(ch, h, mz), psend.at[ch, h], precv.at[ch, h], f, mz
            ).wait_recv()

        arrived(0)
        ring(ch, 1, piece(ch, 0, mz), mz, 0, 0, mr).start()
        ring(ch, 1, piece(ch, 0, mz), mz, 0, 3, ml).start()
        arrived(1)
        ring(ch, 1, piece(ch, 1, mz), mz, 1, 2, ml).start()
        ring(ch, 1, piece(ch, 1, mz), mz, 1, 1, mr).start()

    def base(r):
        return (z if r == 0 else 1 - z) * 4

    def arrived(ch, r, mm, h, n):
        ring(ch, r, piece(ch, h, base(r) + mm), base(r) + mm, h, n, mr).wait_recv()

    def gather_relay(ch, r):
        arrived(ch, r, xl, 0, 0)
        ring(ch, r, piece(ch, 0, base(r) + xl), base(r) + xl, 0, 4, mr).start()
        arrived(ch, r, xr, 1, 2)
        ring(ch, r, piece(ch, 1, base(r) + xr), base(r) + xr, 1, 5, ml).start()

    def weights(i):
        j = shard_of(i)

        def block(a, _):
            rows = pl.ds(pl.multiple_of(a * 256, 256), 256)
            left = jnp.dot(norm_t[rows, :], back[i], preferred_element_type=F32).astype(BF)
            grads[j, a, :, :, :, 0:384] = left.reshape(4, 2, 32, 384)
            left = jnp.dot(og_t[rows, :], ao[i], preferred_element_type=F32).astype(BF)
            grads[j, a, :, :, :, 384:512] = left.reshape(4, 2, 32, 128)
            return 0

        lax.fori_loop(0, 4, block, 0)
        y_far(i, 0).start()
        y_far(i, 1).start()

    def y_far(i, h):
        src = grads.at[shard_of(i), pl.ds(2 * h, 2), yf]
        return remote(src, gf.at[i, h], y1send.at[i, h], y1recv.at[i, h], fr if h == 0 else fl, m)

    def y_near(i, h):
        src = grads.at[shard_of(i), :, yr if h == 0 else yl]
        return remote(src, gn.at[i, h], y2send.at[i, h], y2recv.at[i, h], fr if h == 0 else fl, m)

    def y_step(i, _):
        j = shard_of(i)
        for h in range(2):
            y_far(i, h).wait_recv()
            to = yr if h == 0 else yl
            for a in range(2):
                total = grads[j, 2 * h + a, to].astype(F32) + gf[i, h, a].astype(F32)
                grads[j, 2 * h + a, to] = total.astype(BF)
            y_near(i, h).start()
        return 0

    def z_copy(i, n):
        to = ((n // 2) * 4 + y) * 2 + n % 2
        return remote(gz.at[i, n], gzr.at[i, zi], zsend.at[i, n], zrecv.at[i, zi], to, c * 4 + x)

    def zg_copy(n):
        to = ((n // 2) * 4 + y) * 2 + n % 2
        return remote(gzg.at[n], gzgr.at[zi], zsend.at[4, n], zrecv.at[4, zi], to, c * 4 + x)

    def z_self(n):
        return jnp.logical_and(n == zh * 2 + c, own)

    def own_z(i):
        return pltpu.make_async_copy(gz.at[i, zh * 2 + c], gzr.at[i, zi], zloc.at[i])

    def own_zg():
        return pltpu.make_async_copy(gzg.at[zh * 2 + c], gzgr.at[zi], zloc.at[4])

    def z_step(i, _):
        j = shard_of(i)
        for h in range(2):
            y_near(i, h).wait_recv()
        for a in range(4):
            total = grads[j, a, y].astype(F32) + (gn[i, 0, a].astype(F32) + gn[i, 1, a].astype(F32))
            gz[i, 2 * a : 2 * a + 2] = total.astype(BF)

        def z_send(n, _):
            @pl.when(jnp.logical_not(z_self(n)))
            def _():
                z_copy(i, n).start()

            return 0

        lax.fori_loop(0, 8, z_send, 0)

        @pl.when(own)
        def _():
            own_z(i).start()

        return 0

    def z_wait(i, src, dst):
        def wait(n, _):
            @pl.when(jnp.logical_not(jnp.logical_and(n == zi, own)))
            def _():
                remote(src, dst(n), zsend.at[i, 0], zrecv.at[i, n], f, m).wait_recv()

            return 0

        lax.fori_loop(0, 8, wait, 0)

    def sum8(terms):
        while len(terms) > 1:
            terms = [a + b for a, b in zip(terms[::2], terms[1::2])]
        return terms[0]

    def x_copy(i):
        return remote(gxs.at[i], gxr.at[i], xsend.at[i], xrecv.at[i], f, z * 4 + shard_of(i))

    def x_step(i, _):
        z_wait(i, gz.at[0, 0], lambda n: gzr.at[i, n])

        @pl.when(own)
        def _():
            own_z(i).wait()

        gxs[i] = sum8([gzr[i, k].astype(F32) for k in range(8)]).astype(BF)

        @pl.when(i > 0)
        def _():
            x_copy(i).start()

        return 0

    def gain_y(k):
        yk = (y + k) % 4
        return remote(gcol.at[:, yk], ggr.at[k], gsend.at[k], grecv.at[k], (zh * 4 + yk) * 2 + c, m)

    own_gain = pltpu.make_async_copy(gcol.at[:, y], ggr.at[0], gloc)

    def gain_x(k):
        return remote(gxg, gxgr.at[k], hsend.at[k], hrecv.at[k], f, z * 4 + (x + k) % 4)

    to_sib_gain = remote(gvec, gvecr, vsend, vrecv, sib, m)

    tokens_arrived(0)
    prepare(0)

    @pl.when(own)
    def _():
        own_w.wait()

    def first_heads(i, _):
        @pl.when(i > 0)
        def _():
            slot = shard_of(i)

            @pl.when(i != 2)
            def _():
                for h in range(2):
                    @pl.when(jnp.logical_or(h == 1, i == 3))
                    def _():
                        remote(wown.at[half[h]], wout.at[slot, half[h]], wsend.at[0], wrecv.at[i, h], f, mr).wait_recv()

            @pl.when(i == 2)
            def _():
                remote(wown.at[half[0]], wout.at[slot, half[0]], wsend.at[0], wrecv.at[i, 0], f, mr).wait_recv()

        heads(0, i)
        return 0

    lax.fori_loop(0, 4, first_heads, 0)
    partial(0)
    relay_tokens(1)
    token_gradient(0)

    tokens_arrived(1)
    prepare(1)

    def second_heads(i, _):
        @pl.when(i == 2)
        def _():
            gather_own(0)

        heads(1, i)
        return 0

    lax.fori_loop(0, 4, second_heads, 0)
    partial(1)
    gather_pair(0)
    token_gradient(1)
    gvec[...] = jnp.broadcast_to(jnp.sum(gacc[...], axis=0, keepdims=True), (8, D))
    to_sib_gain.start()
    gather_relay(0, 0)

    def all_weights(i, _):
        weights(i)

        @pl.when(i == 2)
        def _():
            gather_relay(0, 1)

        return 0

    lax.fori_loop(0, 4, all_weights, 0)
    gather_own(1)
    to_sib_gain.wait_recv()
    gcol[...] = jnp.broadcast_to(gvec[0:1] + gvecr[0:1], (128, D)).T.astype(BF).reshape(4, 4, 2, 32, 128)
    for k in range(1, 4):
        gain_y(k).start()
    own_gain.start()
    lax.fori_loop(0, 4, y_step, 0)
    gather_pair(1)
    lax.fori_loop(0, 4, z_step, 0)
    gather_relay(1, 0)

    own_gain.wait()
    for k in range(1, 4):
        remote(ggr.at[0], ggr.at[k], gsend.at[k], grecv.at[k], f, m).wait_recv()
    total = sum8([ggr[k].astype(F32) for k in range(4)])
    gzg[...] = total.astype(BF).reshape(8, 32, 128)

    def zg_send(n, _):
        @pl.when(jnp.logical_not(z_self(n)))
        def _():
            zg_copy(n).start()

        return 0

    lax.fori_loop(0, 8, zg_send, 0)

    @pl.when(own)
    def _():
        own_zg().start()

    lax.fori_loop(0, 4, x_step, 0)
    z_wait(4, gzg.at[0], lambda n: gzgr.at[n])

    @pl.when(own)
    def _():
        own_zg().wait()

    gxg[...] = sum8([gzgr[k].astype(F32) for k in range(8)]).astype(BF)
    for k in range(1, 4):
        gain_x(k).start()
    gather_relay(1, 1)

    for i in range(1, 4):
        x_copy(i).wait_recv()
    total = sum8([gxs[0].astype(F32)] + [gxr[i].astype(F32) for i in range(1, 4)])
    for j in range(3):
        gq[j] = total[:, 128 * j : 128 * j + 128]
    go[...] = total[:, 384:512]
    for k in range(1, 4):
        gain_x(k).wait_recv()
    total = sum8([gxg[...].astype(F32)] + [gxgr[k].astype(F32) for k in range(1, 4)])
    gg[...] = jnp.broadcast_to(total[0:32, 0:1], (32, 128))

    for ch in range(2):
        for r in range(2):
            arrived(ch, r, xl, 1, 1)
            arrived(ch, r, xr, 0, 3)
            arrived(ch, r, xf, 0, 4)
            arrived(ch, r, xf, 1, 5)
            for n, (mm, h) in enumerate(((x, 0), (x, 1), (x, 1), (x, 0), (xl, 0), (xr, 1))):
                ring(ch, r, piece(ch, h, base(r) + mm), base(r) + mm, h, n, mr).wait_send()
        pair(ch, 0).wait_send()
        pair(ch, 1).wait_send()
        own_out(ch).wait()
        to_sibling(ch).wait_send()

        def sent(k, _, ch=ch):
            a2a(ch, k).wait_send()
            back_to(ch, k).wait_send()
            forward(ch, k, recv.at[ch, c, (g + 16 - k) % 16]).wait_send()
            return 0

        lax.fori_loop(1, 16, sent, 0)
        forward(ch, 0, sbuf.at[ch, g]).wait_send()
    to_sib_gain.wait_send()
    for n in range(6):
        i, h = w_pairs[n]
        w_ring(wown.at[half[h]], x, n, mr).wait_send()

    @pl.when(jnp.logical_not(own))
    def _():
        swap(0).wait_send()
        swap(1).wait_send()

    for k in range(1, 4):
        gain_y(k).wait_send()
        gain_x(k).wait_send()
        x_copy(k).wait_send()

    def y_sent(i, _):
        for h in range(2):
            y_far(i, h).wait_send()
            y_near(i, h).wait_send()
        return 0

    lax.fori_loop(0, 4, y_sent, 0)

    def z_sent(n, _):
        @pl.when(jnp.logical_not(z_self(n)))
        def _():
            for i in range(4):
                z_copy(i, n).wait_send()
            zg_copy(n).wait_send()

        return 0

    lax.fori_loop(0, 8, z_sent, 0)


def sublayer(tok, og, qkvw, outw, gain):
    vm = pl.BlockSpec(memory_space=pltpu.VMEM)
    hbm = pl.BlockSpec(memory_space=pltpu.HBM)
    dma = pltpu.SemaphoreType.DMA
    perms = [jnp.asarray(p, BF) for p in (PACK, GROUP, REPACK, UNPACK)]
    bf = lambda *shape: pltpu.VMEM(shape, BF)
    return pl.pallas_call(
        sublayer_kernel,
        out_shape=(
            jax.ShapeDtypeStruct((12, 256, D), BF),
            jax.ShapeDtypeStruct((3, 32, 128), F32),
            jax.ShapeDtypeStruct((32, 128), F32),
            jax.ShapeDtypeStruct((32, 128), F32),
        ),
        in_specs=[hbm] * 4 + [vm] * 5,
        out_specs=(hbm, vm, vm, vm),
        scratch_shapes=[
            bf(2, 2, 6, 32, D),
            bf(2, 16, 48, 512),
            bf(2, 2, 16, 48, 512),
            bf(D, 512),
            bf(4, D, 512),
            bf(4, 384, D),
            bf(128, D),
            bf(2, 2, 6, 2, 32, D),
            bf(768, D),
            bf(D, 768),
            bf(D, 768),
            bf(384, 512),
            bf(4, 768, 384),
            bf(4, 768, 128),
            pltpu.VMEM((6, 2, 32, D), F32),
            bf(2, 6, 32, D),
            bf(2, 6, 32, D),
            bf(6, 32, D),
            pltpu.VMEM((8, D), F32),
            pltpu.VMEM((8, D), F32),
            pltpu.VMEM((8, D), F32),
            bf(4, 4, 2, 32, 128),
            bf(2, 16, 48, 256),
            bf(2, 16, 48, 256),
            bf(2, 6, 32, D),
            bf(4, 4, 4, 2, 32, 512),
            bf(4, 2, 2, 2, 32, 512),
            bf(4, 2, 4, 2, 32, 512),
            bf(4, 4, 2, 32, 128),
            bf(4, 8, 32, 512),
            bf(4, 8, 32, 512),
            bf(8, 32, 128),
            bf(8, 32, 128),
            bf(4, 32, 512),
            bf(4, 32, 512),
            bf(32, 128),
            bf(4, 32, 128),
            dma((8,)),
            dma((4,)),
            dma,
            dma((2,)),
            dma((5,)),
            dma,
            dma((2, 16)),
            dma((2, 16)),
            dma((2, 16)),
            dma((2, 16)),
            dma((2,)),
            dma((2,)),
            dma((6,)),
            dma((4, 2)),
            dma((2,)),
            dma((2,)),
            dma,
            dma,
            dma((2, 16)),
            dma((2, 16)),
            dma((2, 2)),
            dma((2, 2)),
            dma((2, 2, 6)),
            dma((2, 2, 6)),
            dma((4, 2)),
            dma((4, 2)),
            dma((4, 2)),
            dma((4, 2)),
            dma((4,)),
            dma((4,)),
            dma((5, 8)),
            dma((5, 8)),
            dma((4,)),
            dma((4,)),
            dma((4,)),
            dma((4,)),
        ],
        compiler_params=pltpu.CompilerParams(
            collective_id=0, has_side_effects=True, vmem_limit_bytes=57 * 2**20
        ),
        name="sublayer",
    )(tok, og, qkvw, outw, gain, *perms)


def shards(tokens, output_gradient, gain, qkv_weight, out_weight):
    clips, frames, patches, width = tokens.shape
    tgrad, gq, go, gg = sublayer(
        tokens.reshape(12, 256, D),
        output_gradient.reshape(12, 256, D),
        jnp.transpose(qkv_weight, (1, 0, 2)),
        out_weight,
        gain.reshape(1, D),
    )
    return (
        tgrad.reshape(clips, frames, patches, width),
        jnp.transpose(gq, (1, 0, 2)),
        go.T,
        gg[:, 0],
    )


def solution(mesh):
    in_specs = (
        P(None, "frame", None, None),
        P(None, "frame", None, None),
        P(),
        P(None, None, "mlp"),
        P("mlp", None),
    )
    out_specs = (
        P(None, "frame", None, None),
        P("frame", None, "mlp"),
        P("mlp", "frame"),
        P("frame"),
    )
    return jax.shard_map(shards, mesh=mesh, in_specs=in_specs, out_specs=out_specs, check_vma=False)
```

time: 612 us -> 171 us (0.28); the launches traced: 601 us -> 171 us
  waiting for transfers between devices: 351 us -> 0 us
  Pallas kernels: 0 us -> 162 us
  local copies, waits for them, and re-layouts: 81.4 us -> 8.78 us
  starting transfers between devices: 58.5 us -> 0 us
  matrix products: 56.8 us -> 0 us
  other arithmetic: 36.8 us -> 0 us
  between operations: 15.8 us -> 0.64 us
    reduce_scatter x2 -> x0, waiting for transfers between devices: 175 us -> none  [the longest x1 102 us: shards(): lax.psum_scatter(jnp.dot(rows2.T, dstack, preferred_element_type=jnp.floa...]
    pallas_call x0 -> x1, Pallas kernels: none -> 162 us  [sublayer(): pl.pallas_call(sublayer_kernel, out_shape=(jax.ShapeDtypeStruct((12, 256,...]
    all_to_all x8 -> x0, waiting for transfers between devices: 102 us -> none  [the longest x1 20.7 us: shards(): lax.all_to_all(proj[:, :, :, 0], 'frame', split_axis=2, concat_axis=1, ti...]
    unnamed x5 -> x0, waiting for transfers between devices: 73.9 us -> none
    all_to_all x8 -> x0, starting transfers between devices: 58.1 us -> none  [the longest x1 12.8 us: shards(): lax.all_to_all(d_attn, 'frame', split_axis=2, concat_axis=1, tiled=True)]
    dot_general x10 -> x0, matrix products: 52.4 us -> none  [the longest x1 7.25 us: shards(): jnp.dot(rows2.T, dstack, preferred_element_type=jnp.float32)]
    reshape x15 -> x0, local copies, waits for them, and re-layouts: 42.4 us -> none  [the longest x8 21.8 us: shards(): piece.reshape(count, frames, patch_loc, heads_loc, HD)]
    convert_element_type x4 -> x0, other arithmetic: 19.3 us -> none  [the longest x1 12 us: norm_backward(): (output_gradient.astype(jnp.float32) + inverse_deviation * inner_product)...]
  transfers between devices with their start and end apart: 12 -> 0, of which waited for: 10 -> 0; matrix products, arithmetic and copies ran while one was open for 21% -> 0% of each run, Pallas kernels for 0% -> 0%
where the time goes in v2:
time: 171 us
  Pallas kernels  162 us (95%)
  local copies, waits for them, and re-layouts  8.78 us (5%)
    pallas_call x1, Pallas kernels, sublayer(): pl.pallas_call(sublayer_kernel, out_shape=(jax.ShapeDtypeStruct((12, 256,...  162 us
    unnamed x7, local copies, waits for them, and re-layouts  7.43 us

profile of v2, /device:TPU:1, one launch (start us, length us, event | category | flops | bytes accessed | tf_op | source)
XLA Modules:
  0.0 171.2 jit_solution(8097284359771798620)
XLA Ops:
  0.6 161.8 %sublayer.1 = (bf16[12,256,1024]{2,1,0:T(8,128)(2,1)}, f32[3,32,128]{2,1,0:T(8,128)}, f32[32,128]{1,0:T(8,128)}, f32[32,128]{1,0:T(8,128)}) custom-call(bf16[12,256,1024]{2,1,0:T(8,128)(2,1)} %bitcast.7, bf16[12,256,1024]{2,1,0:T(8,128)(2,1)} %bitcast.8, bf16[3,1024,128]{2,1,0:T(8,128)(2,1)} %bitcast.10, bf16[128,1024]{1,0:T(8,128)(2,1)} %outw.1, ...), custom_call_target="tpu_custom_call" | custom-call | tf_op jit(solution)/shard_map/sublayer/pallas_call | solution.py:691
  162.5 1.3 slice_reduce_fusion
  163.8 0.0 copy-start
  163.8 0.0 copy-start.1
  163.8 6.2 %copy.16 = bf16[6,2,256,1024]{3,2,1,0:T(8,128)(2,1)} copy(bf16[6,2,256,1024]{3,2,1,0:T(8,128)(2,1)} %bitcast.9) | data formatting | bytes 12582912
  170.0 0.0 copy-done
  170.0 0.6 copy.17
  170.6 0.0 copy-done.1
  170.6 0.6 copy.18
Async XLA Ops:
  163.8 6.2 %copy-start = (f32[3,32,128]{2,1,0:T(8,128)S(1)}, f32[3,32,128]{2,1,0:T(8,128)}, u32[]{:S(2)}) copy-start(f32[3,32,128]{2,1,0:T(8,128)} %get-tuple-element.9) | copy-start | bytes 147460
  163.8 6.8 %copy-start.1 = (f32[32,128]{1,0:T(8,128)S(1)}, f32[32,128]{1,0:T(8,128)}, u32[]{:S(2)}) copy-start(f32[32,128]{1,0:T(8,128)} %get-tuple-element.10) | copy-start | bytes 49156

commit v3 on v2

--- a/solution.py
+++ b/solution.py
@@ -97,40 +97,61 @@
     yl, yr, yf = (y + 3) % 4, (y + 1) % 4, (y + 2) % 4
     fr, fl = (zh * 4 + yr) * 2 + c, (zh * 4 + yl) * 2 + c
     own = c == z
-    rows32 = pl.ds(pl.multiple_of(m * 32, 32), 32)
-
-    w_in = [pltpu.make_async_copy(qkvw.at[j], wown.at[:, pl.ds(128 * j, 128)], loc.at[4 + j]) for j in range(3)]
-    w_in.append(pltpu.make_async_copy(outw, ow, loc.at[7]))
+    start = (zi + 5 + 3 * z) % 8
+    me = (3 - 3 * z) * 4 + y
+
+    def window(lo, h):
+        return (zh + 3 - 2 * lo + h) % 4
+
+    def owner(slot):
+        to = (start + slot // 4) % 8
+        return ((to // 2) * 4 + slot % 4) * 2 + c, (to % 2) * 4 + x
+
+    def source(n):
+        there = n // 4
+        d = (there + 4 - zh) % 4
+        lo = (d % 2) * (d // 2) + (1 - d % 2) * ((d // 2) * (1 - z) + (1 - d // 2) * z)
+        place = (zi + 16 - (there * 2 + lo + 5 + 3 * lo)) % 8
+        return n * 2 + c, lo * 4 + x, place * 4 + y
+
+    w_in = [pltpu.make_async_copy(qkvw.at[j], wown.at[:, pl.ds(128 * j, 128)], loc.at[j]) for j in range(3)]
+    w_in.append(pltpu.make_async_copy(outw, ow, loc.at[3]))
     for copy in w_in:
         copy.start()
     x_in = []
     for ch in range(2):
         for t, ref in enumerate((tok, og)):
-            x_in.append(
-                pltpu.make_async_copy(ref.at[pl.ds(6 * ch, 6), rows32, :], xin.at[ch, t], loc.at[2 * ch + t])
-            )
-            x_in[-1].start()
+            for h in range(2):
+                rows = pl.ds(pl.multiple_of(x * 64 + window(z, h) * 16, 16), 16)
+                x_in.append(
+                    pltpu.make_async_copy(
+                        ref.at[pl.ds(6 * ch, 6), rows, :],
+                        xin.at[ch, t, :, pl.ds(16 * h, 16), :],
+                        loc.at[4 + 4 * ch + 2 * t + h],
+                    )
+                )
+                x_in[-1].start()
 
     barrier = pltpu.get_barrier_semaphore()
 
-    def hello_frame(k, _):
-        greet(barrier, ((g + k) % 16) * 2 + c, m)
-        return 0
-
-    def hello_column(k, _):
-        dz = (zi + k // 2) % 8
-        greet(barrier, ((dz // 2) * 4 + y) * 2 + (c + k) % 2, (dz % 2) * 4 + x)
-        return 0
-
-    lax.fori_loop(1, 16, hello_frame, 0)
-    lax.fori_loop(1, 16, hello_column, 0)
+    def hello_plane(k, _):
+        n = (zi * 4 + y + k) % 32
+        greet(barrier, ((n // 8) * 4 + n % 4) * 2 + c, ((n // 4) % 2) * 4 + x)
+        return 0
+
+    def hello_other(k, _):
+        greet(barrier, ((k // 2) * 4 + y) * 2 + 1 - c, (k % 2) * 4 + x)
+        return 0
+
+    lax.fori_loop(1, 32, hello_plane, 0)
+    lax.fori_loop(0, 8, hello_other, 0)
     for k in range(1, 4):
         greet(barrier, f, z * 4 + (x + k) % 4)
 
     for copy in w_in:
         copy.wait()
     wown[:, 384:512] = ow[...].T
-    pl.semaphore_wait(barrier, 33)
+    pl.semaphore_wait(barrier, 42)
 
     half = (pl.ds(0, 512), pl.ds(512, 512))
     w_pairs = ((1, 0), (1, 1), (2, 1), (2, 0), (3, 0), (3, 1))
@@ -170,19 +191,19 @@
         swap(1).start()
 
     def a2a(ch, k):
-        to = (g + k) % 16
-        return remote(sbuf.at[ch, to], recv.at[ch, c, g], asend.at[ch, k], arecv.at[ch, k], to * 2 + c, m)
+        slot = (me + k) % 16
+        return remote(sbuf.at[ch, slot], recv.at[ch, c, g], asend.at[ch, k], arecv.at[ch, g], *owner(slot))
 
     def forward(ch, k, src):
         slot = (g + 16 - k) % 16
         return remote(src, recv.at[ch, c, slot], fsend.at[ch, k], frecv.at[ch, k], sib, m)
 
     def keep(ch):
-        return pltpu.make_async_copy(sbuf.at[ch, g], recv.at[ch, c, g], kloc.at[ch])
+        return pltpu.make_async_copy(sbuf.at[ch, me], recv.at[ch, c, g], kloc.at[ch])
 
     for ch in range(2):
-        x_in[2 * ch].wait()
-        x_in[2 * ch + 1].wait()
+        for copy in x_in[4 * ch : 4 * ch + 4]:
+            copy.wait()
         for gh in range(2):
             rows = slice(16 * gh, 16 * gh + 16)
             parts = [xin[ch, t, :, rows, 512 * h : 512 * h + 512].reshape(96, 512) for h in range(2) for t in range(2)]
@@ -195,7 +216,7 @@
 
         lax.fori_loop(1, 16, send, 0)
         keep(ch).start()
-        forward(ch, 0, sbuf.at[ch, g]).start()
+        forward(ch, 0, sbuf.at[ch, me]).start()
 
     @pl.when(jnp.logical_not(own))
     def _():
@@ -212,7 +233,7 @@
     def relay_tokens(ch):
         def relay(k, _):
             slot = (g + 16 - k) % 16
-            remote(sbuf.at[ch, 0], recv.at[ch, c, slot], asend.at[ch, k], arecv.at[ch, k], f, m).wait_recv()
+            remote(sbuf.at[ch, 0], recv.at[ch, c, slot], asend.at[ch, k], arecv.at[ch, slot], f, m).wait_recv()
             forward(ch, k, recv.at[ch, c, slot]).start()
             return 0
 
@@ -295,11 +316,12 @@
         to_sibling(ch).start()
 
     def back_to(ch, k):
-        to = (g + k) % 16
-        return remote(sret.at[ch, to], rret.at[ch, g], csend.at[ch, k], crecv.at[ch, k], to * 2 + c, m)
+        n = (g + k) % 16
+        fs, ms, slot = source(n)
+        return remote(sret.at[ch, n], rret.at[ch, slot], csend.at[ch, k], crecv.at[ch, slot], fs, ms)
 
     def keep_back(ch):
-        return pltpu.make_async_copy(sret.at[ch, g], rret.at[ch, g], kloc.at[2 + ch])
+        return pltpu.make_async_copy(sret.at[ch, g], rret.at[ch, me], kloc.at[2 + ch])
 
     def token_gradient(ch):
         to_sibling(ch).wait_recv()
@@ -330,29 +352,28 @@
         lax.fori_loop(1, 16, send, 0)
         keep_back(ch).start()
 
-    def span(mm):
-        return pl.ds(pl.multiple_of(mm * 32, 32), 32)
-
     def piece(ch, h, mm):
-        return tgrad.at[pl.ds(6 * ch + 3 * h, 3), span(mm), :]
+        rows = pl.ds(pl.multiple_of((mm % 4) * 64 + window(mm // 4, h) * 16, 16), 16)
+        return tgrad.at[pl.ds(6 * ch, 6), rows, :]
+
+    def kept(ch, h):
+        return blk.at[ch, :, pl.ds(16 * h, 16), :]
 
     def pair(ch, h):
-        return remote(
-            blk.at[ch, pl.ds(3 * h, 3)], piece(ch, h, m), psend.at[ch, h], precv.at[ch, h], f, mz
-        )
+        return remote(kept(ch, h), piece(ch, h, m), psend.at[ch, h], precv.at[ch, h], f, mz)
 
     def ring(ch, r, src, mm, h, n, to):
         return remote(src, piece(ch, h, mm), rsend.at[ch, r, n], rrecv.at[ch, r, n], f, to)
 
-    def own_out(ch):
-        return pltpu.make_async_copy(blk.at[ch], tgrad.at[pl.ds(6 * ch, 6), span(m), :], oloc.at[ch])
+    def own_out(ch, h):
+        return pltpu.make_async_copy(kept(ch, h), piece(ch, h, m), oloc.at[ch, h])
 
     def gather_own(ch):
         keep_back(ch).wait()
 
         def received(k, _):
-            slot = (g + 16 - k) % 16
-            remote(sret.at[ch, 0], rret.at[ch, slot], csend.at[ch, k], crecv.at[ch, k], f, m).wait_recv()
+            slot = (me + k) % 16
+            remote(sret.at[ch, 0], rret.at[ch, slot], csend.at[ch, k], crecv.at[ch, slot], f, m).wait_recv()
             return 0
 
         lax.fori_loop(1, 16, received, 0)
@@ -363,18 +384,16 @@
                 blk[ch, :, 16 * gh : 16 * gh + 16, 256 * h : 256 * h + 256] = rows[h]
         pair(ch, 0).start()
         pair(ch, 1).start()
-        mine = [blk.at[ch, pl.ds(3 * h, 3)] for h in range(2)]
-        ring(ch, 0, mine[0], m, 0, 0, mr).start()
-        ring(ch, 0, mine[1], m, 1, 2, ml).start()
-        ring(ch, 0, mine[1], m, 1, 1, mr).start()
-        ring(ch, 0, mine[0], m, 0, 3, ml).start()
-        own_out(ch).start()
+        ring(ch, 0, kept(ch, 0), m, 0, 0, mr).start()
+        ring(ch, 0, kept(ch, 1), m, 1, 2, ml).start()
+        ring(ch, 0, kept(ch, 1), m, 1, 1, mr).start()
+        ring(ch, 0, kept(ch, 0), m, 0, 3, ml).start()
+        own_out(ch, 0).start()
+        own_out(ch, 1).start()
 
     def gather_pair(ch):
         def arrived(h):
-            remote(
-                blk.at[ch, pl.ds(3 * h, 3)], piece(ch, h, mz), psend.at[ch, h], precv.at[ch, h], f, mz
-            ).wait_recv()
+            remote(kept(ch, h), piece(ch, h, mz), psend.at[ch, h], precv.at[ch, h], f, mz).wait_recv()
 
         arrived(0)
         ring(ch, 1, piece(ch, 0, mz), mz, 0, 0, mr).start()
@@ -521,27 +540,25 @@
         own_w.wait()
 
     def first_heads(i, _):
+        @pl.when(i == 3)
+        def _():
+            relay_tokens(1)
+
         @pl.when(i > 0)
         def _():
             slot = shard_of(i)
-
-            @pl.when(i != 2)
-            def _():
-                for h in range(2):
-                    @pl.when(jnp.logical_or(h == 1, i == 3))
-                    def _():
-                        remote(wown.at[half[h]], wout.at[slot, half[h]], wsend.at[0], wrecv.at[i, h], f, mr).wait_recv()
-
-            @pl.when(i == 2)
-            def _():
-                remote(wown.at[half[0]], wout.at[slot, half[0]], wsend.at[0], wrecv.at[i, 0], f, mr).wait_recv()
+            for h in range(2):
+                waited = jnp.logical_and(i < 3, h == i - 1)
+
+                @pl.when(jnp.logical_not(waited))
+                def _():
+                    remote(wown.at[half[h]], wout.at[slot, half[h]], wsend.at[0], wrecv.at[i, h], f, mr).wait_recv()
 
         heads(0, i)
         return 0
 
     lax.fori_loop(0, 4, first_heads, 0)
     partial(0)
-    relay_tokens(1)
     token_gradient(0)
 
     tokens_arrived(1)
@@ -556,32 +573,30 @@
         return 0
 
     lax.fori_loop(0, 4, second_heads, 0)
+    gather_pair(0)
+
+    def all_weights(i, _):
+        weights(i)
+        return 0
+
+    lax.fori_loop(0, 4, all_weights, 0)
+    lax.fori_loop(0, 2, y_step, 0)
     partial(1)
-    gather_pair(0)
+    gather_relay(0, 0)
+    lax.fori_loop(2, 4, y_step, 0)
     token_gradient(1)
     gvec[...] = jnp.broadcast_to(jnp.sum(gacc[...], axis=0, keepdims=True), (8, D))
     to_sib_gain.start()
-    gather_relay(0, 0)
-
-    def all_weights(i, _):
-        weights(i)
-
-        @pl.when(i == 2)
-        def _():
-            gather_relay(0, 1)
-
-        return 0
-
-    lax.fori_loop(0, 4, all_weights, 0)
-    gather_own(1)
+    gather_relay(0, 1)
     to_sib_gain.wait_recv()
     gcol[...] = jnp.broadcast_to(gvec[0:1] + gvecr[0:1], (128, D)).T.astype(BF).reshape(4, 4, 2, 32, 128)
     for k in range(1, 4):
         gain_y(k).start()
     own_gain.start()
-    lax.fori_loop(0, 4, y_step, 0)
+    lax.fori_loop(0, 2, z_step, 0)
+    gather_own(1)
+    lax.fori_loop(2, 4, z_step, 0)
     gather_pair(1)
-    lax.fori_loop(0, 4, z_step, 0)
     gather_relay(1, 0)
 
     own_gain.wait()
@@ -636,7 +651,8 @@
                 ring(ch, r, piece(ch, h, base(r) + mm), base(r) + mm, h, n, mr).wait_send()
         pair(ch, 0).wait_send()
         pair(ch, 1).wait_send()
-        own_out(ch).wait()
+        own_out(ch, 0).wait()
+        own_out(ch, 1).wait()
         to_sibling(ch).wait_send()
 
         def sent(k, _, ch=ch):
@@ -646,7 +662,7 @@
             return 0
 
         lax.fori_loop(1, 16, sent, 0)
-        forward(ch, 0, sbuf.at[ch, g]).wait_send()
+        forward(ch, 0, sbuf.at[ch, me]).wait_send()
     to_sib_gain.wait_send()
     for n in range(6):
         i, h = w_pairs[n]
@@ -736,10 +752,10 @@
             bf(4, 32, 512),
             bf(32, 128),
             bf(4, 32, 128),
-            dma((8,)),
+            dma((12,)),
             dma((4,)),
             dma,
-            dma((2,)),
+            dma((2, 2)),
             dma((5,)),
             dma,
             dma((2, 16)),

time: 171 us -> 172 us (level)
  no operation moved by 1% of the time
where the time goes in v3:
time: 172 us
  Pallas kernels  162 us (94%)
  local copies, waits for them, and re-layouts  8.78 us (5%)
    pallas_call x1, Pallas kernels, sublayer(): pl.pallas_call(sublayer_kernel, out_shape=(jax.ShapeDtypeStruct((12, 256,...  162 us
    unnamed x7, local copies, waits for them, and re-layouts  7.43 us

profile of v3, /device:TPU:1, one launch (start us, length us, event | category | flops | bytes accessed | tf_op | source)
XLA Modules:
  0.0 171.6 jit_solution(12086913580863967005)
XLA Ops:
  0.6 162.2 %sublayer.1 = (bf16[12,256,1024]{2,1,0:T(8,128)(2,1)}, f32[3,32,128]{2,1,0:T(8,128)}, f32[32,128]{1,0:T(8,128)}, f32[32,128]{1,0:T(8,128)}) custom-call(bf16[12,256,1024]{2,1,0:T(8,128)(2,1)} %bitcast.7, bf16[12,256,1024]{2,1,0:T(8,128)(2,1)} %bitcast.8, bf16[3,1024,128]{2,1,0:T(8,128)(2,1)} %bitcast.10, bf16[128,1024]{1,0:T(8,128)(2,1)} %outw.1, ...), custom_call_target="tpu_custom_call" | custom-call | tf_op jit(solution)/shard_map/sublayer/pallas_call | solution.py:707
  162.9 1.3 slice_reduce_fusion
  164.2 0.0 copy-start
  164.2 0.0 copy-start.1
  164.2 6.2 %copy.16 = bf16[6,2,256,1024]{3,2,1,0:T(8,128)(2,1)} copy(bf16[6,2,256,1024]{3,2,1,0:T(8,128)(2,1)} %bitcast.9) | data formatting | bytes 12582912
  170.4 0.0 copy-done
  170.4 0.6 copy.17
  171.0 0.0 copy-done.1
  171.0 0.6 copy.18
Async XLA Ops:
  164.2 6.2 %copy-start = (f32[3,32,128]{2,1,0:T(8,128)S(1)}, f32[3,32,128]{2,1,0:T(8,128)}, u32[]{:S(2)}) copy-start(f32[3,32,128]{2,1,0:T(8,128)} %get-tuple-element.9) | copy-start | bytes 147460
  164.2 6.8 %copy-start.1 = (f32[32,128]{1,0:T(8,128)S(1)}, f32[32,128]{1,0:T(8,128)}, u32[]{:S(2)}) copy-start(f32[32,128]{1,0:T(8,128)} %get-tuple-element.10) | copy-start | bytes 49156

commit v4 on v3

--- a/solution.py
+++ b/solution.py
@@ -539,65 +539,71 @@
     def _():
         own_w.wait()
 
+    def shard_arrived(i):
+        for h in range(2):
+            waited = jnp.logical_or(i == 0, jnp.logical_and(i < 3, h == i - 1))
+
+            @pl.when(jnp.logical_not(waited))
+            def _():
+                slot = shard_of(i)
+                remote(wown.at[half[h]], wout.at[slot, half[h]], wsend.at[0], wrecv.at[i, h], f, mr).wait_recv()
+
     def first_heads(i, _):
+        shard_arrived(i)
+        heads(0, i)
+        return 0
+
+    def second_heads(i, _):
+        heads(1, i)
+        return 0
+
+    def both_heads(i, _):
+        shard_arrived(i)
+        heads(0, i)
+
         @pl.when(i == 3)
         def _():
-            relay_tokens(1)
-
-        @pl.when(i > 0)
-        def _():
-            slot = shard_of(i)
-            for h in range(2):
-                waited = jnp.logical_and(i < 3, h == i - 1)
-
-                @pl.when(jnp.logical_not(waited))
-                def _():
-                    remote(wown.at[half[h]], wout.at[slot, half[h]], wsend.at[0], wrecv.at[i, h], f, mr).wait_recv()
-
-        heads(0, i)
-        return 0
-
-    lax.fori_loop(0, 4, first_heads, 0)
-    partial(0)
-    token_gradient(0)
-
+            partial(0)
+
+        heads(1, i)
+        return 0
+
+    def all_weights(i, _):
+        weights(i)
+        return 0
+
+    lax.fori_loop(0, 2, first_heads, 0)
+    relay_tokens(1)
     tokens_arrived(1)
     prepare(1)
-
-    def second_heads(i, _):
-        @pl.when(i == 2)
-        def _():
-            gather_own(0)
-
-        heads(1, i)
-        return 0
-
-    lax.fori_loop(0, 4, second_heads, 0)
+    lax.fori_loop(0, 2, second_heads, 0)
+    lax.fori_loop(2, 4, both_heads, 0)
+    token_gradient(0)
+    lax.fori_loop(0, 2, all_weights, 0)
+    gather_own(0)
+    lax.fori_loop(2, 4, all_weights, 0)
+    partial(1)
+    y_step(0, 0)
     gather_pair(0)
-
-    def all_weights(i, _):
-        weights(i)
-        return 0
-
-    lax.fori_loop(0, 4, all_weights, 0)
-    lax.fori_loop(0, 2, y_step, 0)
-    partial(1)
-    gather_relay(0, 0)
-    lax.fori_loop(2, 4, y_step, 0)
     token_gradient(1)
     gvec[...] = jnp.broadcast_to(jnp.sum(gacc[...], axis=0, keepdims=True), (8, D))
     to_sib_gain.start()
-    gather_relay(0, 1)
+    lax.fori_loop(1, 3, y_step, 0)
+    gather_relay(0, 0)
+    y_step(3, 0)
     to_sib_gain.wait_recv()
     gcol[...] = jnp.broadcast_to(gvec[0:1] + gvecr[0:1], (128, D)).T.astype(BF).reshape(4, 4, 2, 32, 128)
     for k in range(1, 4):
         gain_y(k).start()
     own_gain.start()
-    lax.fori_loop(0, 2, z_step, 0)
     gather_own(1)
-    lax.fori_loop(2, 4, z_step, 0)
+    z_step(0, 0)
+    gather_relay(0, 1)
+    z_step(1, 0)
     gather_pair(1)
+    z_step(2, 0)
     gather_relay(1, 0)
+    z_step(3, 0)
 
     own_gain.wait()
     for k in range(1, 4):
@@ -713,7 +719,7 @@
             jax.ShapeDtypeStruct((32, 128), F32),
         ),
         in_specs=[hbm] * 4 + [vm] * 5,
-        out_specs=(hbm, vm, vm, vm),
+        out_specs=(pl.BlockSpec(memory_space=pl.ANY), vm, vm, vm),
         scratch_shapes=[
             bf(2, 2, 6, 32, D),
             bf(2, 16, 48, 512),
@@ -790,7 +796,7 @@
             dma((4,)),
         ],
         compiler_params=pltpu.CompilerParams(
-            collective_id=0, has_side_effects=True, vmem_limit_bytes=57 * 2**20
+            collective_id=0, has_side_effects=True, vmem_limit_bytes=46 * 2**20
         ),
         name="sublayer",
     )(tok, og, qkvw, outw, gain, *perms)

time: 172 us -> 170 us (0.988)
  Pallas kernels: 162 us -> 155 us
  local copies, waits for them, and re-layouts: 8.78 us -> 14.7 us
    pallas_call x1, Pallas kernels: 162 us -> 155 us  [sublayer(): pl.pallas_call(sublayer_kernel, out_shape=(jax.ShapeDtypeStruct((12, 256,...]
    unnamed x7 -> x17, local copies, waits for them, and re-layouts: 7.43 us -> 14 us
where the time goes in v4:
time: 170 us
  Pallas kernels  155 us (91%)
  local copies, waits for them, and re-layouts  14.7 us (9%)
    pallas_call x1, Pallas kernels, sublayer(): pl.pallas_call(sublayer_kernel, out_shape=(jax.ShapeDtypeStruct((12, 256,...  155 us
    unnamed x17, local copies, waits for them, and re-layouts  14 us

profile of v4, /device:TPU:1, one launch (start us, length us, event | category | flops | bytes accessed | tf_op | source)
XLA Modules:
  0.0 170.1 jit_solution(11747953269609628314)
XLA Ops:
  0.6 0.0 copy-start
  0.6 1.1 copy-done
  1.8 0.0 copy-start.1
  1.8 1.0 copy-done.1
  2.7 0.0 copy-start.2
  2.7 1.0 copy-done.2
  3.7 0.0 copy-start.3
  3.7 1.0 copy-done.3
  4.7 0.0 copy-start.4
  4.7 1.0 copy-done.4
  5.6 0.0 copy-start.5
  5.6 0.9 copy-done.5
  6.6 0.0 copy-start.6
  6.6 0.7 copy-done.6
  7.3 154.8 %sublayer.1 = (bf16[12,256,1024]{2,1,0:T(8,128)(2,1)}, f32[3,32,128]{2,1,0:T(8,128)S(1)}, f32[32,128]{1,0:T(8,128)S(1)}, f32[32,128]{1,0:T(8,128)S(1)}) custom-call(bf16[12,256,1024]{2,1,0:T(8,128)(2,1)} %bitcast.11, bf16[12,256,1024]{2,1,0:T(8,128)(2,1)} %bitcast.12, bf16[3,1024,128]{2,1,0:T(8,128)(2,1)S(1)} %bitcast.7, bf16[128,1024]{1,0:T(8,128)(2,1)S(1)} %copy-done.5, ...), custom_call_target="tpu_custom_call" | custom-call | tf_op jit(solution)/shard_map/sublayer/pallas_call | solution.py:713
  162.1 0.6 slice_reduce_fusion
  162.7 6.2 %copy.16 = bf16[6,2,256,1024]{3,2,1,0:T(8,128)(2,1)} copy(bf16[6,2,256,1024]{3,2,1,0:T(8,128)(2,1)} %bitcast.13) | data formatting | bytes 12582912
  168.9 0.6 copy.17
  169.5 0.6 copy.18
Async XLA Ops:
  0.6 1.1 copy-start
  1.8 1.0 copy-start.1
  2.7 1.0 copy-start.2
  3.7 1.0 copy-start.3
  4.7 1.0 copy-start.4
  5.6 0.9 copy-start.5
  6.6 0.7 copy-start.6

commit v5 on v4

--- a/solution.py
+++ b/solution.py
@@ -46,8 +46,8 @@
     return lax.dot_general(a, b, (((1,), (1,)), ((), ())), preferred_element_type=F32)
 
 
-def t_dot(a, b):
-    return lax.dot_general(a, b, (((0,), (0,)), ((), ())), preferred_element_type=F32)
+def turned(a):
+    return jnp.concatenate([a[:, :128].T, a[:, 128:].T], axis=1)
 
 
 def attend(q, k, v, d, allowed, first):
@@ -69,19 +69,19 @@
     dscore = jnp.concatenate(dscore, axis=1)
     out = jnp.dot(probs, v2, preferred_element_type=F32)
     dq = jnp.dot(dscore, k2, preferred_element_type=F32)
-    dv = t_dot(probs, d)
-    dk = t_dot(dscore, q)
-    dv = jnp.where(first, dv[:128], dv[128:])
-    dk = jnp.where(first, dk[:128], dk[128:])
+    d2 = jnp.concatenate([jnp.where(first, d, zero), jnp.where(first, zero, d)], axis=0)
+    q2 = jnp.concatenate([jnp.where(first, q, zero), jnp.where(first, zero, q)], axis=0)
+    dv = jnp.dot(turned(probs), d2, preferred_element_type=F32)
+    dk = jnp.dot(turned(dscore), q2, preferred_element_type=F32)
     return out, dq, dk, dv
 
 
 def sublayer_kernel(
-    tok, og, qkvw, outw, gain, pack_p, group_p, repack_p, unpack_p,
+    tok, og, qkvw, outw, gain, perms,
     tgrad, gq, go, gg,
-    xin, sbuf, recv, wown, wout, wt, ow, xs, normed, norm_t, og_t, proj, back, ao, part, other, rsib,
+    order, xin, sbuf, recv, wown, wout, wt, ow, xs, normed, norm_t, og_t, proj, back, ao, part, other, rsib,
     tg, gacc, gvec, gvecr, gcol, sret, rret, blk, grads, gf, gn, ggr, gz, gzr, gzg, gzgr, gxs, gxr, gxg, gxgr,
-    loc, kloc, wloc, oloc, zloc, gloc,
+    loc, ploc, kloc, wloc, oloc, zloc, gloc,
     asend, arecv, fsend, frecv, ssend, srecv, wsend, wrecv, bsend, brecv, vsend, vrecv,
     csend, crecv, psend, precv, rsend, rrecv, y1send, y1recv, y2send, y2recv, gsend, grecv,
     zsend, zrecv, xsend, xrecv, hsend, hrecv,
@@ -114,6 +114,9 @@
         place = (zi + 16 - (there * 2 + lo + 5 + 3 * lo)) % 8
         return n * 2 + c, lo * 4 + x, place * 4 + y
 
+    p_in = [pltpu.make_async_copy(perms.at[pl.ds(0, 1)], order.at[pl.ds(0, 1)], ploc.at[0])]
+    p_in.append(pltpu.make_async_copy(perms.at[pl.ds(1, 3)], order.at[pl.ds(1, 3)], ploc.at[1]))
+    p_in[0].start()
     w_in = [pltpu.make_async_copy(qkvw.at[j], wown.at[:, pl.ds(128 * j, 128)], loc.at[j]) for j in range(3)]
     w_in.append(pltpu.make_async_copy(outw, ow, loc.at[3]))
     for copy in w_in:
@@ -132,6 +135,7 @@
                 )
                 x_in[-1].start()
 
+    p_in[1].start()
     barrier = pltpu.get_barrier_semaphore()
 
     def hello_plane(k, _):
@@ -151,6 +155,18 @@
     for copy in w_in:
         copy.wait()
     wown[:, 384:512] = ow[...].T
+    p_in[0].wait()
+
+    def pack(ch):
+        for copy in x_in[4 * ch : 4 * ch + 4]:
+            copy.wait()
+        for gh in range(2):
+            rows = slice(16 * gh, 16 * gh + 16)
+            parts = [xin[ch, t, :, rows, 512 * h : 512 * h + 512].reshape(96, 512) for h in range(2) for t in range(2)]
+            packed = jnp.dot(order[0], jnp.concatenate(parts, axis=0), preferred_element_type=F32)
+            sbuf[ch, 8 * gh : 8 * gh + 8] = packed.astype(BF).reshape(8, 48, 512)
+
+    pack(0)
     pl.semaphore_wait(barrier, 42)
 
     half = (pl.ds(0, 512), pl.ds(512, 512))
@@ -168,14 +184,8 @@
             w_ring(src.at[half[1]], x, 2, ml).start()
             w_ring(src.at[half[1]], x, 1, mr).start()
 
-    far = (zi + 7 + 2 * z) % 8
-    near_id = (g * 2 + 1 - c, mz)
-    far_id = (((far // 2) * 4 + y) * 2 + 1 - c, (far % 2) * 4 + x)
-
     def swap(h):
-        return remote(
-            wown.at[half[h]], wout.at[x, half[h]], ssend.at[h], srecv.at[h], *(near_id if h == 0 else far_id)
-        )
+        return remote(wown.at[half[h]], wout.at[x, half[h]], ssend.at[h], srecv.at[h], g * 2 + 1 - c, mz)
 
     own_w = pltpu.make_async_copy(wown, wout.at[x], wloc)
 
@@ -202,13 +212,8 @@
         return pltpu.make_async_copy(sbuf.at[ch, me], recv.at[ch, c, g], kloc.at[ch])
 
     for ch in range(2):
-        for copy in x_in[4 * ch : 4 * ch + 4]:
-            copy.wait()
-        for gh in range(2):
-            rows = slice(16 * gh, 16 * gh + 16)
-            parts = [xin[ch, t, :, rows, 512 * h : 512 * h + 512].reshape(96, 512) for h in range(2) for t in range(2)]
-            packed = jnp.dot(pack_p[...], jnp.concatenate(parts, axis=0), preferred_element_type=F32)
-            sbuf[ch, 8 * gh : 8 * gh + 8] = packed.astype(BF).reshape(8, 48, 512)
+        if ch:
+            pack(ch)
 
         def send(k, _, ch=ch):
             a2a(ch, k).start()
@@ -267,7 +272,7 @@
         for s in range(2):
             for gh in range(2):
                 block = recv[ch, s, 8 * gh : 8 * gh + 8].reshape(384, 512)
-                rows = jnp.dot(group_p[...], block, preferred_element_type=F32).astype(BF).reshape(2, 2, 6, 16, 512)
+                rows = jnp.dot(order[1], block, preferred_element_type=F32).astype(BF).reshape(2, 2, 6, 16, 512)
                 for h in range(2):
                     xs[ch, :, :, s, 16 * gh : 16 * gh + 16, 512 * h : 512 * h + 512] = rows[h]
 
@@ -342,7 +347,7 @@
         for gh in range(2):
             rows = slice(16 * gh, 16 * gh + 16)
             parts = [tg[:, rows, 256 * h : 256 * h + 256].reshape(96, 256) for h in range(4)]
-            packed = jnp.dot(repack_p[...], jnp.concatenate(parts, axis=0), preferred_element_type=F32)
+            packed = jnp.dot(order[2], jnp.concatenate(parts, axis=0), preferred_element_type=F32)
             sret[ch, 8 * gh : 8 * gh + 8] = packed.astype(BF).reshape(8, 48, 256)
 
         def send(k, _):
@@ -379,7 +384,7 @@
         lax.fori_loop(1, 16, received, 0)
         for gh in range(2):
             block = rret[ch, 8 * gh : 8 * gh + 8].reshape(384, 256)
-            rows = jnp.dot(unpack_p[...], block, preferred_element_type=F32).astype(BF).reshape(4, 6, 16, 256)
+            rows = jnp.dot(order[3], block, preferred_element_type=F32).astype(BF).reshape(4, 6, 16, 256)
             for h in range(4):
                 blk[ch, :, 16 * gh : 16 * gh + 16, 256 * h : 256 * h + 256] = rows[h]
         pair(ch, 0).start()
@@ -532,6 +537,55 @@
 
     to_sib_gain = remote(gvec, gvecr, vsend, vrecv, sib, m)
 
+    def sent_early():
+        for ch in range(2):
+            pair(ch, 0).wait_send()
+            pair(ch, 1).wait_send()
+            own_out(ch, 0).wait()
+            own_out(ch, 1).wait()
+            to_sibling(ch).wait_send()
+
+            def sent(k, _, ch=ch):
+                a2a(ch, k).wait_send()
+                back_to(ch, k).wait_send()
+                forward(ch, k, recv.at[ch, c, (g + 16 - k) % 16]).wait_send()
+                return 0
+
+            lax.fori_loop(1, 16, sent, 0)
+            forward(ch, 0, sbuf.at[ch, me]).wait_send()
+        to_sib_gain.wait_send()
+        for n in range(6):
+            i, h = w_pairs[n]
+            w_ring(wown.at[half[h]], x, n, mr).wait_send()
+
+        @pl.when(jnp.logical_not(own))
+        def _():
+            swap(0).wait_send()
+            swap(1).wait_send()
+
+        for k in range(1, 4):
+            gain_y(k).wait_send()
+
+        def y_sent(i, _):
+            for h in range(2):
+                y_far(i, h).wait_send()
+                y_near(i, h).wait_send()
+            return 0
+
+        lax.fori_loop(0, 4, y_sent, 0)
+
+        def z_sent(n, _):
+            @pl.when(jnp.logical_not(z_self(n)))
+            def _():
+                for i in range(4):
+                    z_copy(i, n).wait_send()
+                zg_copy(n).wait_send()
+
+            return 0
+
+        lax.fori_loop(0, 8, z_sent, 0)
+
+    p_in[1].wait()
     tokens_arrived(0)
     prepare(0)
 
@@ -551,37 +605,35 @@
     def first_heads(i, _):
         shard_arrived(i)
         heads(0, i)
+
+        @pl.when(i == 2)
+        def _():
+            relay_tokens(1)
+            tokens_arrived(1)
+            prepare(1)
+            heads(1, 0)
+
         return 0
 
     def second_heads(i, _):
         heads(1, i)
-        return 0
-
-    def both_heads(i, _):
-        shard_arrived(i)
-        heads(0, i)
-
-        @pl.when(i == 3)
+
+        @pl.when(i == 1)
         def _():
-            partial(0)
-
-        heads(1, i)
+            token_gradient(0)
+
         return 0
 
     def all_weights(i, _):
         weights(i)
         return 0
 
-    lax.fori_loop(0, 2, first_heads, 0)
-    relay_tokens(1)
-    tokens_arrived(1)
-    prepare(1)
-    lax.fori_loop(0, 2, second_heads, 0)
-    lax.fori_loop(2, 4, both_heads, 0)
-    token_gradient(0)
-    lax.fori_loop(0, 2, all_weights, 0)
+    lax.fori_loop(0, 4, first_heads, 0)
+    partial(0)
+    lax.fori_loop(1, 4, second_heads, 0)
+    lax.fori_loop(0, 1, all_weights, 0)
     gather_own(0)
-    lax.fori_loop(2, 4, all_weights, 0)
+    lax.fori_loop(1, 4, all_weights, 0)
     partial(1)
     y_step(0, 0)
     gather_pair(0)
@@ -634,6 +686,7 @@
     gxg[...] = sum8([gzgr[k].astype(F32) for k in range(8)]).astype(BF)
     for k in range(1, 4):
         gain_x(k).start()
+    sent_early()
     gather_relay(1, 1)
 
     for i in range(1, 4):
@@ -655,60 +708,16 @@
             arrived(ch, r, xf, 1, 5)
             for n, (mm, h) in enumerate(((x, 0), (x, 1), (x, 1), (x, 0), (xl, 0), (xr, 1))):
                 ring(ch, r, piece(ch, h, base(r) + mm), base(r) + mm, h, n, mr).wait_send()
-        pair(ch, 0).wait_send()
-        pair(ch, 1).wait_send()
-        own_out(ch, 0).wait()
-        own_out(ch, 1).wait()
-        to_sibling(ch).wait_send()
-
-        def sent(k, _, ch=ch):
-            a2a(ch, k).wait_send()
-            back_to(ch, k).wait_send()
-            forward(ch, k, recv.at[ch, c, (g + 16 - k) % 16]).wait_send()
-            return 0
-
-        lax.fori_loop(1, 16, sent, 0)
-        forward(ch, 0, sbuf.at[ch, me]).wait_send()
-    to_sib_gain.wait_send()
-    for n in range(6):
-        i, h = w_pairs[n]
-        w_ring(wown.at[half[h]], x, n, mr).wait_send()
-
-    @pl.when(jnp.logical_not(own))
-    def _():
-        swap(0).wait_send()
-        swap(1).wait_send()
-
     for k in range(1, 4):
-        gain_y(k).wait_send()
         gain_x(k).wait_send()
         x_copy(k).wait_send()
-
-    def y_sent(i, _):
-        for h in range(2):
-            y_far(i, h).wait_send()
-            y_near(i, h).wait_send()
-        return 0
-
-    lax.fori_loop(0, 4, y_sent, 0)
-
-    def z_sent(n, _):
-        @pl.when(jnp.logical_not(z_self(n)))
-        def _():
-            for i in range(4):
-                z_copy(i, n).wait_send()
-            zg_copy(n).wait_send()
-
-        return 0
-
-    lax.fori_loop(0, 8, z_sent, 0)
 
 
 def sublayer(tok, og, qkvw, outw, gain):
     vm = pl.BlockSpec(memory_space=pltpu.VMEM)
     hbm = pl.BlockSpec(memory_space=pltpu.HBM)
     dma = pltpu.SemaphoreType.DMA
-    perms = [jnp.asarray(p, BF) for p in (PACK, GROUP, REPACK, UNPACK)]
+    perms = jnp.asarray(np.stack([PACK, GROUP, REPACK, UNPACK]), BF)
     bf = lambda *shape: pltpu.VMEM(shape, BF)
     return pl.pallas_call(
         sublayer_kernel,
@@ -718,9 +727,10 @@
             jax.ShapeDtypeStruct((32, 128), F32),
             jax.ShapeDtypeStruct((32, 128), F32),
         ),
-        in_specs=[hbm] * 4 + [vm] * 5,
-        out_specs=(pl.BlockSpec(memory_space=pl.ANY), vm, vm, vm),
+        in_specs=[hbm] * 4 + [vm, hbm],
+        out_specs=(hbm, vm, vm, vm),
         scratch_shapes=[
+            bf(4, 384, 384),
             bf(2, 2, 6, 32, D),
             bf(2, 16, 48, 512),
             bf(2, 2, 16, 48, 512),
@@ -759,6 +769,7 @@
             bf(32, 128),
             bf(4, 32, 128),
             dma((12,)),
+            dma((2,)),
             dma((4,)),
             dma,
             dma((2, 2)),
@@ -796,10 +807,10 @@
             dma((4,)),
         ],
         compiler_params=pltpu.CompilerParams(
-            collective_id=0, has_side_effects=True, vmem_limit_bytes=46 * 2**20
+            collective_id=0, has_side_effects=True, vmem_limit_bytes=58 * 2**20
         ),
         name="sublayer",
-    )(tok, og, qkvw, outw, gain, *perms)
+    )(tok, og, qkvw, outw, gain, perms)
 
 
 def shards(tokens, output_gradient, gain, qkv_weight, out_weight):

time: 170 us -> 162 us (0.953)
  local copies, waits for them, and re-layouts: 14.7 us -> 8.78 us
  Pallas kernels: 155 us -> 153 us
    unnamed x17 -> x7, local copies, waits for them, and re-layouts: 14 us -> 7.43 us
    pallas_call x1, Pallas kernels: 155 us -> 153 us  [sublayer(): pl.pallas_call(sublayer_kernel, out_shape=(jax.ShapeDtypeStruct((12, 256,...]
where the time goes in v5:
time: 162 us
  Pallas kernels  153 us (94%)
  local copies, waits for them, and re-layouts  8.78 us (5%)
    pallas_call x1, Pallas kernels, sublayer(): pl.pallas_call(sublayer_kernel, out_shape=(jax.ShapeDtypeStruct((12, 256,...  153 us
    unnamed x7, local copies, waits for them, and re-layouts  7.43 us

profile of v5, /device:TPU:1, one launch (start us, length us, event | category | flops | bytes accessed | tf_op | source)
XLA Modules:
  0.0 162.0 jit_solution(4538813170189782789)
XLA Ops:
  0.6 152.6 %sublayer.1 = (bf16[12,256,1024]{2,1,0:T(8,128)(2,1)}, f32[3,32,128]{2,1,0:T(8,128)}, f32[32,128]{1,0:T(8,128)}, f32[32,128]{1,0:T(8,128)}) custom-call(bf16[12,256,1024]{2,1,0:T(8,128)(2,1)} %bitcast.7, bf16[12,256,1024]{2,1,0:T(8,128)(2,1)} %bitcast.8, bf16[3,1024,128]{2,1,0:T(8,128)(2,1)} %bitcast.10, bf16[128,1024]{1,0:T(8,128)(2,1)} %outw.1, ...), custom_call_target="tpu_custom_call" | custom-call | tf_op jit(solution)/shard_map/sublayer/pallas_call | solution.py:722
  153.2 1.3 slice_reduce_fusion
  154.6 0.0 copy-start
  154.6 0.0 copy-start.1
  154.6 6.2 %copy.13 = bf16[6,2,256,1024]{3,2,1,0:T(8,128)(2,1)} copy(bf16[6,2,256,1024]{3,2,1,0:T(8,128)(2,1)} %bitcast.9) | data formatting | bytes 12582912
  160.8 0.0 copy-done
  160.8 0.6 copy.14
  161.4 0.0 copy-done.1
  161.4 0.6 copy.15
Async XLA Ops:
  154.6 6.2 %copy-start = (f32[3,32,128]{2,1,0:T(8,128)S(1)}, f32[3,32,128]{2,1,0:T(8,128)}, u32[]{:S(2)}) copy-start(f32[3,32,128]{2,1,0:T(8,128)} %get-tuple-element.9) | copy-start | bytes 147460
  154.6 6.8 %copy-start.1 = (f32[32,128]{1,0:T(8,128)S(1)}, f32[32,128]{1,0:T(8,128)}, u32[]{:S(2)}) copy-start(f32[32,128]{1,0:T(8,128)} %get-tuple-element.10) | copy-start | bytes 49156

commit v6 on v5

--- a/solution.py
+++ b/solution.py
@@ -82,7 +82,7 @@
     order, xin, sbuf, recv, wown, wout, wt, ow, xs, normed, norm_t, og_t, proj, back, ao, part, other, rsib,
     tg, gacc, gvec, gvecr, gcol, sret, rret, blk, grads, gf, gn, ggr, gz, gzr, gzg, gzgr, gxs, gxr, gxg, gxgr,
     loc, ploc, kloc, wloc, oloc, zloc, gloc,
-    asend, arecv, fsend, frecv, ssend, srecv, wsend, wrecv, bsend, brecv, vsend, vrecv,
+    asend, arecv, fsend, frecv, ssend, srecv, qsend, qrecv, usend, urecv, wsend, wrecv, bsend, brecv, vsend, vrecv,
     csend, crecv, psend, precv, rsend, rrecv, y1send, y1recv, y2send, y2recv, gsend, grecv,
     zsend, zrecv, xsend, xrecv, hsend, hrecv,
 ):
@@ -169,7 +169,8 @@
     pack(0)
     pl.semaphore_wait(barrier, 42)
 
-    half = (pl.ds(0, 512), pl.ds(512, 512))
+    half = (pl.ds(0, 384), pl.ds(384, 384))
+    strip = pl.ds(pl.multiple_of(768 + 64 * y, 64), 64)
     w_pairs = ((1, 0), (1, 1), (2, 1), (2, 0), (3, 0), (3, 1))
 
     def w_ring(src, slot, n, to):
@@ -185,18 +186,33 @@
             w_ring(src.at[half[1]], x, 1, mr).start()
 
     def swap(h):
-        return remote(wown.at[half[h]], wout.at[x, half[h]], ssend.at[h], srecv.at[h], g * 2 + 1 - c, mz)
-
-    own_w = pltpu.make_async_copy(wown, wout.at[x], wloc)
+        rows = (half[0], half[1], strip)[h]
+        return remote(wown.at[rows], wout.at[x, rows], ssend.at[h], srecv.at[h], g * 2 + 1 - c, mz)
+
+    def strip_x(src, k):
+        return remote(src.at[strip], wout.at[x, strip], qsend.at[k], qrecv.at[k], f, z * 4 + (x + k) % 4)
+
+    def strip_y(k):
+        to = (zh * 4 + (y + k) % 4) * 2 + c
+        return remote(wout.at[:, strip], wout.at[:, strip], usend.at[k], urecv.at[k], to, m)
+
+    own_w = [
+        pltpu.make_async_copy(wown.at[pl.ds(0, 768)], wout.at[x, pl.ds(0, 768)], wloc.at[0]),
+        pltpu.make_async_copy(wown.at[strip], wout.at[x, strip], wloc.at[1]),
+    ]
 
     @pl.when(own)
     def _():
+        own_w[1].start()
+        for k in range(1, 4):
+            strip_x(wown, k).start()
         w_spread(wown, 0)
         w_spread(wown, 1)
-        own_w.start()
+        own_w[0].start()
 
     @pl.when(jnp.logical_not(own))
     def _():
+        swap(2).start()
         swap(0).start()
         swap(1).start()
 
@@ -222,6 +238,23 @@
         lax.fori_loop(1, 16, send, 0)
         keep(ch).start()
         forward(ch, 0, sbuf.at[ch, me]).start()
+
+        if ch == 0:
+
+            @pl.when(jnp.logical_not(own))
+            def _():
+                swap(2).wait_recv()
+                for k in range(1, 4):
+                    strip_x(wout.at[x], k).start()
+
+    @pl.when(own)
+    def _():
+        own_w[1].wait()
+
+    for k in range(1, 4):
+        remote(wown.at[strip], wout.at[(x + 4 - k) % 4, strip], qsend.at[k], qrecv.at[k], f, m).wait_recv()
+    for k in range(1, 4):
+        strip_y(k).start()
 
     @pl.when(jnp.logical_not(own))
     def _():
@@ -560,11 +593,13 @@
 
         @pl.when(jnp.logical_not(own))
         def _():
-            swap(0).wait_send()
-            swap(1).wait_send()
+            for h in range(3):
+                swap(h).wait_send()
 
         for k in range(1, 4):
             gain_y(k).wait_send()
+            strip_x(wown, k).wait_send()
+            strip_y(k).wait_send()
 
         def y_sent(i, _):
             for h in range(2):
@@ -591,7 +626,11 @@
 
     @pl.when(own)
     def _():
-        own_w.wait()
+        own_w[0].wait()
+
+    for k in range(1, 4):
+        rows = pl.ds(pl.multiple_of(768 + 64 * ((y + 4 - k) % 4), 64), 64)
+        remote(wout.at[:, rows], wout.at[:, rows], usend.at[k], urecv.at[k], f, m).wait_recv()
 
     def shard_arrived(i):
         for h in range(2):
@@ -631,31 +670,29 @@
     lax.fori_loop(0, 4, first_heads, 0)
     partial(0)
     lax.fori_loop(1, 4, second_heads, 0)
+    partial(1)
     lax.fori_loop(0, 1, all_weights, 0)
-    gather_own(0)
-    lax.fori_loop(1, 4, all_weights, 0)
-    partial(1)
-    y_step(0, 0)
-    gather_pair(0)
     token_gradient(1)
     gvec[...] = jnp.broadcast_to(jnp.sum(gacc[...], axis=0, keepdims=True), (8, D))
     to_sib_gain.start()
-    lax.fori_loop(1, 3, y_step, 0)
+    gather_own(0)
+    lax.fori_loop(1, 4, all_weights, 0)
+    gather_pair(0)
+    lax.fori_loop(0, 2, y_step, 0)
     gather_relay(0, 0)
-    y_step(3, 0)
     to_sib_gain.wait_recv()
     gcol[...] = jnp.broadcast_to(gvec[0:1] + gvecr[0:1], (128, D)).T.astype(BF).reshape(4, 4, 2, 32, 128)
     for k in range(1, 4):
         gain_y(k).start()
     own_gain.start()
     gather_own(1)
-    z_step(0, 0)
+    y_step(2, 0)
+    gather_pair(1)
+    y_step(3, 0)
     gather_relay(0, 1)
-    z_step(1, 0)
-    gather_pair(1)
-    z_step(2, 0)
+    lax.fori_loop(0, 2, z_step, 0)
     gather_relay(1, 0)
-    z_step(3, 0)
+    lax.fori_loop(2, 4, z_step, 0)
 
     own_gain.wait()
     for k in range(1, 4):
@@ -771,7 +808,7 @@
             dma((12,)),
             dma((2,)),
             dma((4,)),
-            dma,
+            dma((2,)),
             dma((2, 2)),
             dma((5,)),
             dma,
@@ -779,8 +816,12 @@
             dma((2, 16)),
             dma((2, 16)),
             dma((2, 16)),
-            dma((2,)),
-            dma((2,)),
+            dma((3,)),
+            dma((3,)),
+            dma((4,)),
+            dma((4,)),
+            dma((4,)),
+            dma((4,)),
             dma((6,)),
             dma((4, 2)),
             dma((2,)),
@@ -813,20 +854,59 @@
     )(tok, og, qkvw, outw, gain, perms)
 
 
+def finish_kernel(tgrad, gq, go, gg, out, oq, oo, og, buf, insem, outsem):
+    into = [pltpu.make_async_copy(tgrad.at[pl.ds(2 * n, 2)], buf.at[pl.ds(2 * n, 2)], insem.at[n]) for n in range(6)]
+    away = [pltpu.make_async_copy(buf.at[pl.ds(2 * n, 2)], out.at[pl.ds(2 * n, 2)], outsem.at[n]) for n in range(6)]
+    for copy in into:
+        copy.start()
+    oq[...] = gq[...]
+    oo[...] = go[...]
+    og[...] = gg[...].T[0:1, :]
+    for n in range(6):
+        into[n].wait()
+        away[n].start()
+    for copy in away:
+        copy.wait()
+
+
+def finish(tgrad, gq, go, gg):
+    vm = pl.BlockSpec(memory_space=pltpu.VMEM)
+    hbm = pl.BlockSpec(memory_space=pltpu.HBM)
+    return pl.pallas_call(
+        finish_kernel,
+        out_shape=(
+            jax.ShapeDtypeStruct((12, 256, D), BF),
+            jax.ShapeDtypeStruct((3, 32, 128), F32),
+            jax.ShapeDtypeStruct((32, 128), F32),
+            jax.ShapeDtypeStruct((1, 32), F32),
+        ),
+        in_specs=[hbm, vm, vm, vm],
+        out_specs=(hbm, vm, vm, vm),
+        scratch_shapes=[
+            pltpu.VMEM((12, 256, D), BF),
+            pltpu.SemaphoreType.DMA((6,)),
+            pltpu.SemaphoreType.DMA((6,)),
+        ],
+        compiler_params=pltpu.CompilerParams(vmem_limit_bytes=58 * 2**20),
+        name="finish",
+    )(tgrad, gq, go, gg)
+
+
 def shards(tokens, output_gradient, gain, qkv_weight, out_weight):
     clips, frames, patches, width = tokens.shape
-    tgrad, gq, go, gg = sublayer(
+    results = sublayer(
         tokens.reshape(12, 256, D),
         output_gradient.reshape(12, 256, D),
         jnp.transpose(qkv_weight, (1, 0, 2)),
         out_weight,
         gain.reshape(1, D),
     )
+    tgrad, gq, go, gg = finish(*results)
     return (
         tgrad.reshape(clips, frames, patches, width),
         jnp.transpose(gq, (1, 0, 2)),
         go.T,
-        gg[:, 0],
+        gg.reshape(32),
     )
 
 

time: 162 us -> 149 us (0.920)
  local copies, waits for them, and re-layouts: 8.78 us -> 0 us
  Pallas kernels: 153 us -> 148 us
    pallas_call x1, Pallas kernels: 153 us -> 141 us  [sublayer(): pl.pallas_call(sublayer_kernel, out_shape=(jax.ShapeDtypeStruct((12, 256,...]
    unnamed x7 -> x0, local copies, waits for them, and re-layouts: 7.43 us -> none
    pallas_call x0 -> x1, Pallas kernels: none -> 6.91 us  [finish(): pl.pallas_call(finish_kernel, out_shape=(jax.ShapeDtypeStruct((12, 256, D...]
where the time goes in v6:
time: 149 us
  Pallas kernels  148 us (99%)
    pallas_call x1, Pallas kernels, sublayer(): pl.pallas_call(sublayer_kernel, out_shape=(jax.ShapeDtypeStruct((12, 256,...  141 us
    pallas_call x1, Pallas kernels, finish(): pl.pallas_call(finish_kernel, out_shape=(jax.ShapeDtypeStruct((12, 256, D...  6.91 us

profile of v6, /device:TPU:1, one launch (start us, length us, event | category | flops | bytes accessed | tf_op | source)
XLA Modules:
  0.0 149.2 jit_solution(2505731652730404417)
XLA Ops:
  0.6 141.5 %sublayer.1 = (bf16[12,256,1024]{2,1,0:T(8,128)(2,1)}, f32[3,32,128]{2,1,0:T(8,128)}, f32[32,128]{1,0:T(8,128)}, f32[32,128]{1,0:T(8,128)}) custom-call(bf16[12,256,1024]{2,1,0:T(8,128)(2,1)} %bitcast.8, bf16[12,256,1024]{2,1,0:T(8,128)(2,1)} %bitcast.9, bf16[3,1024,128]{2,1,0:T(8,128)(2,1)} %bitcast.10, bf16[128,1024]{1,0:T(8,128)(2,1)} %outw.1, ...), custom_call_target="tpu_custom_call" | custom-call | tf_op jit(solution)/shard_map/sublayer/pallas_call | solution.py:759
  142.1 6.9 %finish.1 = (bf16[12,256,1024]{2,1,0:T(8,128)(2,1)}, f32[3,32,128]{2,1,0:T(8,128)}, f32[32,128]{1,0:T(8,128)}, f32[1,32]{1,0:T(1,128)}) custom-call(bf16[12,256,1024]{2,1,0:T(8,128)(2,1)} %get-tuple-element.12.tgrad, f32[3,32,128]{2,1,0:T(8,128)} %get-tuple-element.13.gq, f32[32,128]{1,0:T(8,128)} %get-tuple-element.14.go, f32[32,128]{1,0:T(8,128)} %get-tuple-element.15.gg), custom_call_target="tpu_custom_call" | custom-call | tf_op jit(solution)/shard_map/finish/pallas_call | solution.py:875

commit v7 on v6

--- a/solution.py
+++ b/solution.py
@@ -54,7 +54,8 @@
     zero = jnp.zeros_like(k)
     k2 = jnp.concatenate([jnp.where(first, k, zero), jnp.where(first, zero, k)], axis=0)
     v2 = jnp.concatenate([jnp.where(first, v, zero), jnp.where(first, zero, v)], axis=0)
-    scores = dot_t(q, k2) * FACTOR
+    q = q * FACTOR
+    scores = dot_t(q, k2)
     dprob = dot_t(d, v2)
     probs, dscore = [], []
     for h in range(2):
@@ -64,11 +65,11 @@
         dp = dprob[:, 128 * h : 128 * h + 128]
         delta = jnp.sum(p * dp, axis=-1, keepdims=True)
         probs.append(p.astype(BF))
-        dscore.append((p * (dp - delta) * FACTOR).astype(BF))
+        dscore.append((p * (dp - delta)).astype(BF))
     probs = jnp.concatenate(probs, axis=1)
     dscore = jnp.concatenate(dscore, axis=1)
     out = jnp.dot(probs, v2, preferred_element_type=F32)
-    dq = jnp.dot(dscore, k2, preferred_element_type=F32)
+    dq = jnp.dot(dscore, k2, preferred_element_type=F32) * FACTOR
     d2 = jnp.concatenate([jnp.where(first, d, zero), jnp.where(first, zero, d)], axis=0)
     q2 = jnp.concatenate([jnp.where(first, q, zero), jnp.where(first, zero, q)], axis=0)
     dv = jnp.dot(turned(probs), d2, preferred_element_type=F32)
@@ -314,7 +315,7 @@
             normed[pl.ds(pl.multiple_of(ch * 384 + u * 64, 64), 64), :] = (xhat * gain[...]).astype(BF)
             return 0
 
-        lax.fori_loop(0, 6, norm, 0)
+        lax.fori_loop(0, 6, norm, 0, unroll=2)
         for i in range(3):
             at = 384 * ch + 128 * i
             norm_t[:, at : at + 128] = normed[at : at + 128, :].T
@@ -343,15 +344,20 @@
     def to_sibling(ch):
         return remote(other.at[ch], rsib.at[ch], bsend.at[ch], brecv.at[ch], sib, m)
 
-    def partial(ch):
+    def partial(ch, groups):
         for n in range(3):
             rows = slice(384 * ch + 128 * n, 384 * ch + 128 * n + 128)
-            term = jnp.dot(back[0, rows, :], wt[0], preferred_element_type=F32)
-            for i in range(1, 4):
+            term = jnp.dot(back[groups[0], rows, :], wt[groups[0]], preferred_element_type=F32)
+            for i in groups[1:]:
                 term += jnp.dot(back[i, rows, :], wt[i], preferred_element_type=F32)
-            part[2 * n : 2 * n + 2] = term.reshape(2, 2, 32, D)
-        other[ch] = part[:, 1 - c].astype(BF)
-        to_sibling(ch).start()
+            term = term.reshape(2, 2, 32, D)
+            if groups[0] == 0:
+                part[2 * n : 2 * n + 2] = term
+            else:
+                part[2 * n : 2 * n + 2] += term
+        if groups[-1] == 3:
+            other[ch] = part[:, 1 - c].astype(BF)
+            to_sibling(ch).start()
 
     def back_to(ch, k):
         n = (g + k) % 16
@@ -372,7 +378,7 @@
             tg[u] = (xs[ch, 1, u, c].astype(F32) + rstd * inner).astype(BF)
             return total + jnp.sum((dn * xhat).reshape(4, 8, D), axis=0)
 
-        total = lax.fori_loop(0, 6, token, jnp.zeros((8, D), F32))
+        total = lax.fori_loop(0, 6, token, jnp.zeros((8, D), F32), unroll=2)
         if ch == 0:
             gacc[...] = total
         else:
@@ -455,15 +461,10 @@
     def weights(i):
         j = shard_of(i)
 
-        def block(a, _):
-            rows = pl.ds(pl.multiple_of(a * 256, 256), 256)
-            left = jnp.dot(norm_t[rows, :], back[i], preferred_element_type=F32).astype(BF)
-            grads[j, a, :, :, :, 0:384] = left.reshape(4, 2, 32, 384)
-            left = jnp.dot(og_t[rows, :], ao[i], preferred_element_type=F32).astype(BF)
-            grads[j, a, :, :, :, 384:512] = left.reshape(4, 2, 32, 128)
-            return 0
-
-        lax.fori_loop(0, 4, block, 0)
+        left = jnp.dot(norm_t[...], back[i], preferred_element_type=F32).astype(BF)
+        grads[j, :, :, :, :, 0:384] = left.reshape(4, 4, 2, 32, 384)
+        left = jnp.dot(og_t[...], ao[i], preferred_element_type=F32).astype(BF)
+        grads[j, :, :, :, :, 384:512] = left.reshape(4, 4, 2, 32, 128)
         y_far(i, 0).start()
         y_far(i, 1).start()
 
@@ -553,7 +554,7 @@
 
         gxs[i] = sum8([gzr[i, k].astype(F32) for k in range(8)]).astype(BF)
 
-        @pl.when(i > 0)
+        @pl.when(jnp.asarray(i) > 0)
         def _():
             x_copy(i).start()
 
@@ -647,30 +648,36 @@
 
         @pl.when(i == 2)
         def _():
+            partial(0, (0, 1, 2))
             relay_tokens(1)
-            tokens_arrived(1)
-            prepare(1)
-            heads(1, 0)
 
         return 0
 
     def second_heads(i, _):
         heads(1, i)
 
-        @pl.when(i == 1)
+        @pl.when(i == 0)
         def _():
             token_gradient(0)
 
         return 0
 
     def all_weights(i, _):
-        weights(i)
+        weights((i + 1) % 4)
         return 0
 
+    def y_steps(first, last):
+        lax.fori_loop(first, last, lambda i, _: y_step((i + 1) % 4, 0), 0)
+
+    def z_steps(first, last):
+        lax.fori_loop(first, last, lambda i, _: z_step((i + 1) % 4, 0), 0)
+
     lax.fori_loop(0, 4, first_heads, 0)
-    partial(0)
-    lax.fori_loop(1, 4, second_heads, 0)
-    partial(1)
+    partial(0, (3,))
+    tokens_arrived(1)
+    prepare(1)
+    lax.fori_loop(0, 4, second_heads, 0)
+    partial(1, (0, 1, 2, 3))
     lax.fori_loop(0, 1, all_weights, 0)
     token_gradient(1)
     gvec[...] = jnp.broadcast_to(jnp.sum(gacc[...], axis=0, keepdims=True), (8, D))
@@ -678,7 +685,7 @@
     gather_own(0)
     lax.fori_loop(1, 4, all_weights, 0)
     gather_pair(0)
-    lax.fori_loop(0, 2, y_step, 0)
+    y_steps(0, 2)
     gather_relay(0, 0)
     to_sib_gain.wait_recv()
     gcol[...] = jnp.broadcast_to(gvec[0:1] + gvecr[0:1], (128, D)).T.astype(BF).reshape(4, 4, 2, 32, 128)
@@ -686,13 +693,11 @@
         gain_y(k).start()
     own_gain.start()
     gather_own(1)
-    y_step(2, 0)
+    y_steps(2, 3)
     gather_pair(1)
-    y_step(3, 0)
+    y_steps(3, 4)
     gather_relay(0, 1)
-    lax.fori_loop(0, 2, z_step, 0)
-    gather_relay(1, 0)
-    lax.fori_loop(2, 4, z_step, 0)
+    z_steps(0, 2)
 
     own_gain.wait()
     for k in range(1, 4):
@@ -713,7 +718,9 @@
     def _():
         own_zg().start()
 
-    lax.fori_loop(0, 4, x_step, 0)
+    gather_relay(1, 0)
+    z_steps(2, 4)
+    lax.fori_loop(1, 4, x_step, 0)
     z_wait(4, gzg.at[0], lambda n: gzgr.at[n])
 
     @pl.when(own)
@@ -723,8 +730,9 @@
     gxg[...] = sum8([gzgr[k].astype(F32) for k in range(8)]).astype(BF)
     for k in range(1, 4):
         gain_x(k).start()
+    gather_relay(1, 1)
+    x_step(0, 0)
     sent_early()
-    gather_relay(1, 1)
 
     for i in range(1, 4):
         x_copy(i).wait_recv()

time: 149 us -> 143 us (0.960)
  Pallas kernels: 148 us -> 142 us
    pallas_call x1, Pallas kernels: 141 us -> 135 us  [sublayer(): pl.pallas_call(sublayer_kernel, out_shape=(jax.ShapeDtypeStruct((12, 256,...]
where the time goes in v7:
time: 143 us; the launch traced here: 142 us
  Pallas kernels  142 us (99%)
    pallas_call x1, Pallas kernels, sublayer(): pl.pallas_call(sublayer_kernel, out_shape=(jax.ShapeDtypeStruct((12, 256,...  135 us
    pallas_call x1, Pallas kernels, finish(): pl.pallas_call(finish_kernel, out_shape=(jax.ShapeDtypeStruct((12, 256, D...  6.91 us

profile of v7, /device:TPU:1, one launch (start us, length us, event | category | flops | bytes accessed | tf_op | source)
XLA Modules:
  0.0 142.5 jit_solution(16517669022448083669)
XLA Ops:
  0.6 134.8 %sublayer.1 = (bf16[12,256,1024]{2,1,0:T(8,128)(2,1)}, f32[3,32,128]{2,1,0:T(8,128)}, f32[32,128]{1,0:T(8,128)}, f32[32,128]{1,0:T(8,128)}) custom-call(bf16[12,256,1024]{2,1,0:T(8,128)(2,1)} %bitcast.8, bf16[12,256,1024]{2,1,0:T(8,128)(2,1)} %bitcast.9, bf16[3,1024,128]{2,1,0:T(8,128)(2,1)} %bitcast.10, bf16[128,1024]{1,0:T(8,128)(2,1)} %outw.1, ...), custom_call_target="tpu_custom_call" | custom-call | tf_op jit(solution)/shard_map/sublayer/pallas_call | solution.py:767
  135.4 6.9 %finish.1 = (bf16[12,256,1024]{2,1,0:T(8,128)(2,1)}, f32[3,32,128]{2,1,0:T(8,128)}, f32[32,128]{1,0:T(8,128)}, f32[1,32]{1,0:T(1,128)}) custom-call(bf16[12,256,1024]{2,1,0:T(8,128)(2,1)} %get-tuple-element.12.tgrad, f32[3,32,128]{2,1,0:T(8,128)} %get-tuple-element.13.gq, f32[32,128]{1,0:T(8,128)} %get-tuple-element.14.go, f32[32,128]{1,0:T(8,128)} %get-tuple-element.15.gg), custom_call_target="tpu_custom_call" | custom-call | tf_op jit(solution)/shard_map/finish/pallas_call | solution.py:883

commit v8 on v7

--- a/solution.py
+++ b/solution.py
@@ -662,10 +662,6 @@
 
         return 0
 
-    def all_weights(i, _):
-        weights((i + 1) % 4)
-        return 0
-
     def y_steps(first, last):
         lax.fori_loop(first, last, lambda i, _: y_step((i + 1) % 4, 0), 0)
 
@@ -678,27 +674,30 @@
     prepare(1)
     lax.fori_loop(0, 4, second_heads, 0)
     partial(1, (0, 1, 2, 3))
-    lax.fori_loop(0, 1, all_weights, 0)
+    weights(1)
     token_gradient(1)
     gvec[...] = jnp.broadcast_to(jnp.sum(gacc[...], axis=0, keepdims=True), (8, D))
     to_sib_gain.start()
     gather_own(0)
-    lax.fori_loop(1, 4, all_weights, 0)
+    weights(2)
+    weights(3)
+    weights(0)
     gather_pair(0)
-    y_steps(0, 2)
+    y_steps(0, 1)
+    y_steps(1, 2)
     gather_relay(0, 0)
     to_sib_gain.wait_recv()
     gcol[...] = jnp.broadcast_to(gvec[0:1] + gvecr[0:1], (128, D)).T.astype(BF).reshape(4, 4, 2, 32, 128)
     for k in range(1, 4):
         gain_y(k).start()
     own_gain.start()
+    y_steps(2, 3)
     gather_own(1)
-    y_steps(2, 3)
+    y_steps(3, 4)
+    z_steps(0, 1)
     gather_pair(1)
-    y_steps(3, 4)
+    z_steps(1, 2)
     gather_relay(0, 1)
-    z_steps(0, 2)
-
     own_gain.wait()
     for k in range(1, 4):
         remote(ggr.at[0], ggr.at[k], gsend.at[k], grecv.at[k], f, m).wait_recv()

time: 143 us -> 142 us (level)
  no operation moved by 1% of the time
where the time goes in v8:
time: 142 us
  Pallas kernels  141 us (99%)
    pallas_call x1, Pallas kernels, sublayer(): pl.pallas_call(sublayer_kernel, out_shape=(jax.ShapeDtypeStruct((12, 256,...  135 us
    pallas_call x1, Pallas kernels, finish(): pl.pallas_call(finish_kernel, out_shape=(jax.ShapeDtypeStruct((12, 256, D...  6.91 us

profile of v8, /device:TPU:1, one launch (start us, length us, event | category | flops | bytes accessed | tf_op | source)
XLA Modules:
  0.0 142.3 jit_solution(5987112708583799982)
XLA Ops:
  0.6 134.6 %sublayer.1 = (bf16[12,256,1024]{2,1,0:T(8,128)(2,1)}, f32[3,32,128]{2,1,0:T(8,128)}, f32[32,128]{1,0:T(8,128)}, f32[32,128]{1,0:T(8,128)}) custom-call(bf16[12,256,1024]{2,1,0:T(8,128)(2,1)} %bitcast.8, bf16[12,256,1024]{2,1,0:T(8,128)(2,1)} %bitcast.9, bf16[3,1024,128]{2,1,0:T(8,128)(2,1)} %bitcast.10, bf16[128,1024]{1,0:T(8,128)(2,1)} %outw.1, ...), custom_call_target="tpu_custom_call" | custom-call | tf_op jit(solution)/shard_map/sublayer/pallas_call | solution.py:766
  135.2 6.9 %finish.1 = (bf16[12,256,1024]{2,1,0:T(8,128)(2,1)}, f32[3,32,128]{2,1,0:T(8,128)}, f32[32,128]{1,0:T(8,128)}, f32[1,32]{1,0:T(1,128)}) custom-call(bf16[12,256,1024]{2,1,0:T(8,128)(2,1)} %get-tuple-element.12.tgrad, f32[3,32,128]{2,1,0:T(8,128)} %get-tuple-element.13.gq, f32[32,128]{1,0:T(8,128)} %get-tuple-element.14.go, f32[32,128]{1,0:T(8,128)} %get-tuple-element.15.gg), custom_call_target="tpu_custom_call" | custom-call | tf_op jit(solution)/shard_map/finish/pallas_call | solution.py:882

commit v9 on v8

--- a/solution.py
+++ b/solution.py
@@ -675,11 +675,11 @@
     lax.fori_loop(0, 4, second_heads, 0)
     partial(1, (0, 1, 2, 3))
     weights(1)
+    weights(2)
     token_gradient(1)
     gvec[...] = jnp.broadcast_to(jnp.sum(gacc[...], axis=0, keepdims=True), (8, D))
     to_sib_gain.start()
     gather_own(0)
-    weights(2)
     weights(3)
     weights(0)
     gather_pair(0)

time: 142 us -> 143 us (level)
  no operation moved by 1% of the time
where the time goes in v9:
time: 143 us; the launch traced here: 142 us
  Pallas kernels  141 us (99%)
    pallas_call x1, Pallas kernels, sublayer(): pl.pallas_call(sublayer_kernel, out_shape=(jax.ShapeDtypeStruct((12, 256,...  134 us
    pallas_call x1, Pallas kernels, finish(): pl.pallas_call(finish_kernel, out_shape=(jax.ShapeDtypeStruct((12, 256, D...  6.91 us

profile of v9, /device:TPU:1, one launch (start us, length us, event | category | flops | bytes accessed | tf_op | source)
XLA Modules:
  0.0 142.1 jit_solution(1895615774196956256)
XLA Ops:
  0.6 134.4 %sublayer.1 = (bf16[12,256,1024]{2,1,0:T(8,128)(2,1)}, f32[3,32,128]{2,1,0:T(8,128)}, f32[32,128]{1,0:T(8,128)}, f32[32,128]{1,0:T(8,128)}) custom-call(bf16[12,256,1024]{2,1,0:T(8,128)(2,1)} %bitcast.8, bf16[12,256,1024]{2,1,0:T(8,128)(2,1)} %bitcast.9, bf16[3,1024,128]{2,1,0:T(8,128)(2,1)} %bitcast.10, bf16[128,1024]{1,0:T(8,128)(2,1)} %outw.1, ...), custom_call_target="tpu_custom_call" | custom-call | tf_op jit(solution)/shard_map/sublayer/pallas_call | solution.py:766
  135.1 6.9 %finish.1 = (bf16[12,256,1024]{2,1,0:T(8,128)(2,1)}, f32[3,32,128]{2,1,0:T(8,128)}, f32[32,128]{1,0:T(8,128)}, f32[1,32]{1,0:T(1,128)}) custom-call(bf16[12,256,1024]{2,1,0:T(8,128)(2,1)} %get-tuple-element.12.tgrad, f32[3,32,128]{2,1,0:T(8,128)} %get-tuple-element.13.gq, f32[32,128]{1,0:T(8,128)} %get-tuple-element.14.go, f32[32,128]{1,0:T(8,128)} %get-tuple-element.15.gg), custom_call_target="tpu_custom_call" | custom-call | tf_op jit(solution)/shard_map/finish/pallas_call | solution.py:882
